TPU v7x, 32 devices: a whole 2x2x4 slice. The times are simulated.
32 devices in a mesh: down: 8 (over y, x, core), cross: 4 (over z).
Axes of the slice: x: 2, y: 2, z: 4, core: 2. Of those that a mesh axis runs over, the one named last changes fastest.
Arguments:
- fields: float32 [4, 64, 256, 128], P(None, 'down', 'cross'), may hold values from -4 to 4
- embers: float32 [7, 8, 4, 6, 256], P(None, 'down', 'cross'), may hold values from 0.05 to 1
- counts: int32 [8, 4, 6], P('down', 'cross'), may hold values from 0 to 256, as said below
Outputs:
- advanced: float32 [4, 64, 256, 128], P(None, 'down', 'cross')
- landed: float32 [4, 8, 4, 6, 256], P(None, 'down', 'cross')
Inputs may be any that keep to these rules, and one draw needn't show every extreme that they name: `counts`: live records fill the leading slots of a buffer; some buffer is full in every draw.
All inputs are finite; a program needn't handle non-finite values.
Results may differ from a plain program's by a relative error of at most 0.0003.
Values sent between devices are 32-bit elements; how exact they have to be, the bound alone decides.
A program may use at most 64 MiB of HBM per device.

v0:
```python
import jax
import jax.numpy as jnp
from jax import lax
from jax.sharding import PartitionSpec as P

STEPS = 6


HORIZONTAL_MIX = 0.1
VERTICAL_MIX = 0.1
ADVECTION = 0.25
DRAG_RATE = 0.6
BURN_RATE = 0.5
HEAT_YIELD = 4.0
DESTINATIONS = ((1, -1), (1, 0), (1, 1), (2, -1), (2, 0), (2, 1))


def shifted_2(x, axis, by):
    size = lax.axis_size(axis)
    pairs = [(i, i + by) for i in range(size) if 0 <= i + by < size]
    return lax.ppermute(x, axis, pairs)


def with_halo(x, sides, width):
    for axis, dim in sides:
        size, length = (lax.axis_size(axis), x.shape[dim])
        up = [(i, (i + 1) % size) for i in range(size - 1)]
        down = [(j, i) for i, j in up]
        last = lax.slice_in_dim(x, length - width, length, axis=dim)
        leading = lax.slice_in_dim(x, 0, width, axis=dim)
        before = lax.ppermute(last, axis, up)
        after = lax.ppermute(leading, axis, down)
        x = jnp.concatenate([before, x, after], axis=dim)
    return x


def advance(padded):
    centre = padded[:, 1:-1, 1:-1]
    eastern = padded[:, 2:, 1:-1]
    western = padded[:, :-2, 1:-1]
    northern = padded[:, 1:-1, 2:]
    southern = padded[:, 1:-1, :-2]
    upper_level = jnp.concatenate([centre[..., 1:], centre[..., -1:]], axis=-1)
    lower_level = jnp.concatenate([centre[..., :1], centre[..., :-1]], axis=-1)
    spread = eastern + western + northern + southern - 4.0 * centre
    column_mix = upper_level + lower_level - 2.0 * centre
    carried = centre[0:1] * (eastern - western) * 0.5 + centre[1:2] * (northern - southern) * 0.5
    return centre + HORIZONTAL_MIX * spread + VERTICAL_MIX * column_mix - ADVECTION * carried


def tent_weights(position, cell_count):
    centres = jnp.arange(cell_count).astype(jnp.float32) + 0.5
    return jnp.maximum(0.0, 1.0 - jnp.abs(position[:, None] - centres[None, :]))


def ember_update(tile_fields, records):
    cells_down = tile_fields.shape[1]
    cells_cross = tile_fields.shape[2]
    levels = tile_fields.shape[3]
    weight_down = tent_weights(records[0] * cells_down, cells_down)
    weight_cross = tent_weights(records[1] * cells_cross, cells_cross)
    weight_level = tent_weights(records[2] * levels, levels)
    column = jnp.einsum("kxyz,ez->kxye", tile_fields, weight_level, precision=lax.Precision.HIGHEST)
    across = jnp.sum(column * weight_cross.T[None, None], axis=2)
    sampled = jnp.sum(across * weight_down.T[None], axis=1)
    ember_mass = records[5]
    burned = ember_mass * BURN_RATE * jax.nn.sigmoid(records[6] + sampled[2] - sampled[3])
    living = (ember_mass > 0.0).astype(jnp.float32)
    landed = (
        jnp.stack(
            [
                records[3] + DRAG_RATE * (sampled[0] - records[3]),
                records[4] + DRAG_RATE * (sampled[1] - records[4]),
                records[6] + DRAG_RATE * (sampled[2] - records[6]),
                ember_mass - burned,
            ]
        )
        * living[None]
    )
    spread = (
        weight_down[:, :, None] * weight_cross[:, None, :] * (HEAT_YIELD * burned)[:, None, None]
    )
    spread = spread.reshape(records.shape[1], cells_down * cells_cross)
    deposit = jnp.dot(spread.T, weight_level, precision=lax.Precision.HIGHEST)
    return (landed, deposit.reshape(cells_down, cells_cross, levels))


def local(fields, embers, counts):
    slot_count = embers.shape[3]
    capacity = embers.shape[4]
    slot_index = jnp.arange(capacity)
    live_mask = (slot_index[None, :] < counts[0, 0][:, None]).astype(jnp.float32)
    outgoing = embers[:, 0, 0] * live_mask[None]
    arrived = []
    for target in range(slot_count):
        down_step, cross_step = DESTINATIONS[target]
        shifted = shifted_2(outgoing[:, target], "down", down_step)
        if cross_step != 0:
            shifted = shifted_2(shifted, "cross", cross_step)
        arrived.append(shifted)
    block_rows = 256
    deposit = jnp.zeros(fields.shape[1:], jnp.float32)
    results = []
    for target in range(slot_count):
        records = arrived[target]
        live_count = jnp.sum((records[5] > 0.0).astype(jnp.int32))
        passes = (live_count + block_rows - 1) // block_rows

        def one_pass(iteration, loop_state, records=records):
            finished, heat_sum = loop_state
            updated, extra_heat = ember_update(fields, records)
            return (updated, heat_sum + extra_heat)

        finished, deposit = lax.fori_loop(
            0, passes, one_pass, (jnp.zeros((4, capacity), jnp.float32), deposit)
        )
        results.append(finished)
    landed = jnp.stack(results, axis=1)[:, None, None]
    current = fields
    for step_index in range(STEPS):
        padded = with_halo(current, (("down", 1), ("cross", 2)), 1)
        current = advance(padded)
    advanced = jnp.concatenate([current[:2], current[2:3] + deposit[None], current[3:]], axis=0)
    return (advanced, landed)


def solution(mesh):
    placed = (
        P(None, "down", "cross", None),
        P(None, "down", "cross", None, None),
        P("down", "cross", None),
    )
    return jax.shard_map(
        local,
        mesh=mesh,
        in_specs=placed,
        out_specs=(P(None, "down", "cross", None), P(None, "down", "cross", None, None)),
        check_vma=False,
    )
```

profile of v0, /device:TPU:4, one launch (start us, length us, event | category | flops | bytes accessed | tf_op | source)
XLA Modules:
  0.0 199.6 jit_solution(12052209326867451617)
XLA Ops:
  5.8 3.5 %collective-permute-start.24 = (f32[7,256]{1,0:T(8,128)S(1)}, f32[7,256]{1,0:T(8,128)S(1)}, u32[]{:S(2)}, u32[]{:S(2)}) collective-permute-start(f32[7,256]{1,0:T(8,128)S(1)} %get-tuple-element.1111), channel_id=1, source_target_pairs={{0,4},{4,8},{8,12},{12,16},{16,20},{20,24},{24,28},{1,5},{5,9},{9,... | collective-permute-start | bytes 21512 | tf_op jit(solution)/shard_map/ppermute | solution.py:21
  15.2 2.9 %fusion.174 = (f32[4,8,64,1]{3,2,1,0:T(8,128)S(1)}, f32[4,8,64,1]{3,2,1,0:T(8,128)}) fusion(f32[4,8,64,128]{3,2,1,0:T(8,128)} %param.15), kind=kLoop, calls=%fused_computation.411 | loop fusion | bytes 32768 | tf_op jit(solution)/shard_map/slice | solution.py:44
  27.1 3.5 %collective-permute-start.33 = (f32[7,256]{1,0:T(8,128)S(1)}, f32[7,256]{1,0:T(8,128)S(1)}, u32[]{:S(2)}, u32[]{:S(2)}) collective-permute-start(f32[7,256]{1,0:T(8,128)S(1)} %collective-permute-done.32), channel_id=1, source_target_pairs={{0,1},{1,2},{2,3},{4,5},{5,6},{6,7},{8,9},{9,10},{10,11},{12,13},{... | collective-permute-start | bytes 21512 | tf_op jit(solution)/shard_map/ppermute | solution.py:21
  36.8 4.5 %collective-permute-start.28 = (f32[7,256]{1,0:T(8,128)S(1)}, f32[7,256]{1,0:T(8,128)S(1)}, u32[]{:S(2)}, u32[]{:S(2)}) collective-permute-start(f32[7,256]{1,0:T(8,128)S(1)} %collective-permute-done.27), channel_id=1, source_target_pairs={{0,1},{1,2},{2,3},{4,5},{5,6},{6,7},{8,9},{9,10},{10,11},{12,13},{... | collective-permute-start | bytes 21512 | tf_op jit(solution)/shard_map/ppermute | solution.py:21
  61.0 2.3 %while.96 = (s32[]{:T(128)}, f32[4,256]{1,0:T(4,128)}, f32[8,64,128]{2,1,0:T(8,128)S(1)}, s32[]{:T(128)}, f32[7,256]{1,0:T(8,128)}, /*index=5*/f32[1,256]{1,0:T(...) while((s32[]{:T(128)}, f32[4,256]{1,0:T(4,128)}, ...), condition=%wide.region_4.5_spmd, body=%wide.region_3.4_spmd.sunk | while | flops 72962 | bytes 810093 | solution.py:114
  90.2 5.9 %collective-permute-start.3 = (f32[4,10,1,128]{3,2,1,0:T(1,128)S(1)}, f32[4,10,1,128]{3,2,1,0:T(1,128)S(1)}, u32[]{:S(2)}, u32[]{:S(2)}) collective-permute-start(f32[4,10,1,128]{3,2,1,0:T(1,128)S(1)} %get-tuple-element.1055), channel_id=1, source_target_pairs={{0,1},{1,2},{2,3},{4,5},{5,6},{6,7},{8,9},{9,10},{10,11},{12,13},{... | collective-permute-start | bytes 61448 | tf_op jit(solution)/shard_map/ppermute | solution.py:31
  98.3 3.5 %collective-permute-done.2 = f32[4,10,1,128]{3,2,1,0:T(1,128)S(1)} collective-permute-done((f32[4,10,1,128]{3,2,1,0:T(1,128)S(1)}, f32[4,10,1,128]{3,2,1,0:T(1,128)S(1)}, u32[]{:S(2)}, u32[]{:S(2)}) %collective-permute-start.2) | collective-permute-done | bytes 20512 | tf_op jit(solution)/shard_map/ppermute | solution.py:32
  101.8 2.4 %fusion.15 = f32[4,8,64,128]{3,2,1,0:T(8,128)S(1)} fusion(f32[4,8,64,1]{3,2,1,0:T(8,128)S(1)} %copy-done.1, f32[4,8,64,127]{3,2,1,0:T(8,128)} %get-tuple-element.1105, f32[4,8,64,127]{3,2,1,0:T(8,128)S(1)} %copy-done.2, f32[4,8,64,1]{3,2,1,0:T(8,128)S(1)} %get-tuple-element.1102, f32[4,8,64,128]{3,2,1,0:T(8,128)S(1)} %copy-done, ...), kind=kLoop, calls=%fused_computation.102 | loop fusion | flops 6553600 | bytes 6332416 | tf_op jit(solution)/shard_map/sub | solution.py:48
  106.5 2.4 %collective-permute-start.5 = (f32[4,1,64,128]{3,2,1,0:T(8,128)S(1)}, f32[4,1,64,128]{3,2,1,0:T(8,128)S(1)}, u32[]{:S(2)}, u32[]{:S(2)}) collective-permute-start(f32[4,1,64,128]{3,2,1,0:T(8,128)S(1)} %get-tuple-element.1092), channel_id=1, source_target_pairs={{0,4},{4,8},{8,12},{12,16},{16,20},{20,24},{24,28},{1,5},{5,9},{9,... | collective-permute-start | bytes 393224 | tf_op jit(solution)/shard_map/ppermute | solution.py:31
  109.3 4.4 %collective-permute-done.5 = f32[4,1,64,128]{3,2,1,0:T(8,128)S(1)} collective-permute-done((f32[4,1,64,128]{3,2,1,0:T(8,128)S(1)}, f32[4,1,64,128]{3,2,1,0:T(8,128)S(1)}, u32[]{:S(2)}, u32[]{:S(2)}) %collective-permute-start.5) | collective-permute-done | bytes 131104 | tf_op jit(solution)/shard_map/ppermute | solution.py:31
  113.7 3.5 %collective-permute-start.7 = (f32[4,10,1,128]{3,2,1,0:T(1,128)S(1)}, f32[4,10,1,128]{3,2,1,0:T(1,128)S(1)}, u32[]{:S(2)}, u32[]{:S(2)}) collective-permute-start(f32[4,10,1,128]{3,2,1,0:T(1,128)S(1)} %get-tuple-element.1053), channel_id=1, source_target_pairs={{0,1},{1,2},{2,3},{4,5},{5,6},{6,7},{8,9},{9,10},{10,11},{12,13},{... | collective-permute-start | bytes 61448 | tf_op jit(solution)/shard_map/ppermute | solution.py:31
  118.7 4.2 %collective-permute-done.6 = f32[4,10,1,128]{3,2,1,0:T(1,128)S(1)} collective-permute-done((f32[4,10,1,128]{3,2,1,0:T(1,128)S(1)}, f32[4,10,1,128]{3,2,1,0:T(1,128)S(1)}, u32[]{:S(2)}, u32[]{:S(2)}) %collective-permute-start.6) | collective-permute-done | bytes 20512 | tf_op jit(solution)/shard_map/ppermute | solution.py:32
  126.6 2.4 %collective-permute-start.9 = (f32[4,1,64,128]{3,2,1,0:T(8,128)S(1)}, f32[4,1,64,128]{3,2,1,0:T(8,128)S(1)}, u32[]{:S(2)}, u32[]{:S(2)}) collective-permute-start(f32[4,1,64,128]{3,2,1,0:T(8,128)S(1)} %get-tuple-element.1084), channel_id=1, source_target_pairs={{0,4},{4,8},{8,12},{12,16},{16,20},{20,24},{24,28},{1,5},{5,9},{9,... | collective-permute-start | bytes 393224 | tf_op jit(solution)/shard_map/ppermute | solution.py:31
  129.4 4.4 %collective-permute-done.9 = f32[4,1,64,128]{3,2,1,0:T(8,128)S(1)} collective-permute-done((f32[4,1,64,128]{3,2,1,0:T(8,128)S(1)}, f32[4,1,64,128]{3,2,1,0:T(8,128)S(1)}, u32[]{:S(2)}, u32[]{:S(2)}) %collective-permute-start.9) | collective-permute-done | bytes 131104 | tf_op jit(solution)/shard_map/ppermute | solution.py:31
  137.2 4.2 %collective-permute-done.10 = f32[4,10,1,128]{3,2,1,0:T(1,128)S(1)} collective-permute-done((f32[4,10,1,128]{3,2,1,0:T(1,128)S(1)}, f32[4,10,1,128]{3,2,1,0:T(1,128)S(1)}, u32[]{:S(2)}, u32[]{:S(2)}) %collective-permute-start.10) | collective-permute-done | bytes 20512 | tf_op jit(solution)/shard_map/ppermute | solution.py:32
  145.1 2.4 %collective-permute-start.13 = (f32[4,1,64,128]{3,2,1,0:T(8,128)S(1)}, f32[4,1,64,128]{3,2,1,0:T(8,128)S(1)}, u32[]{:S(2)}, u32[]{:S(2)}) collective-permute-start(f32[4,1,64,128]{3,2,1,0:T(8,128)S(1)} %get-tuple-element.1076), channel_id=1, source_target_pairs={{0,4},{4,8},{8,12},{12,16},{16,20},{20,24},{24,28},{1,5},{5,9},{9,... | collective-permute-start | bytes 393224 | tf_op jit(solution)/shard_map/ppermute | solution.py:31
  147.9 4.4 %collective-permute-done.13 = f32[4,1,64,128]{3,2,1,0:T(8,128)S(1)} collective-permute-done((f32[4,1,64,128]{3,2,1,0:T(8,128)S(1)}, f32[4,1,64,128]{3,2,1,0:T(8,128)S(1)}, u32[]{:S(2)}, u32[]{:S(2)}) %collective-permute-start.13) | collective-permute-done | bytes 131104 | tf_op jit(solution)/shard_map/ppermute | solution.py:31
  155.7 4.2 %collective-permute-done.14 = f32[4,10,1,128]{3,2,1,0:T(1,128)S(1)} collective-permute-done((f32[4,10,1,128]{3,2,1,0:T(1,128)S(1)}, f32[4,10,1,128]{3,2,1,0:T(1,128)S(1)}, u32[]{:S(2)}, u32[]{:S(2)}) %collective-permute-start.14) | collective-permute-done | bytes 20512 | tf_op jit(solution)/shard_map/ppermute | solution.py:32
  163.7 2.4 %collective-permute-start.17 = (f32[4,1,64,128]{3,2,1,0:T(8,128)S(1)}, f32[4,1,64,128]{3,2,1,0:T(8,128)S(1)}, u32[]{:S(2)}, u32[]{:S(2)}) collective-permute-start(f32[4,1,64,128]{3,2,1,0:T(8,128)S(1)} %get-tuple-element.1068), channel_id=1, source_target_pairs={{0,4},{4,8},{8,12},{12,16},{16,20},{20,24},{24,28},{1,5},{5,9},{9,... | collective-permute-start | bytes 393224 | tf_op jit(solution)/shard_map/ppermute | solution.py:31
  166.5 4.4 %collective-permute-done.17 = f32[4,1,64,128]{3,2,1,0:T(8,128)S(1)} collective-permute-done((f32[4,1,64,128]{3,2,1,0:T(8,128)S(1)}, f32[4,1,64,128]{3,2,1,0:T(8,128)S(1)}, u32[]{:S(2)}, u32[]{:S(2)}) %collective-permute-start.17) | collective-permute-done | bytes 131104 | tf_op jit(solution)/shard_map/ppermute | solution.py:31
  174.3 4.2 %collective-permute-done.18 = f32[4,10,1,128]{3,2,1,0:T(1,128)S(1)} collective-permute-done((f32[4,10,1,128]{3,2,1,0:T(1,128)S(1)}, f32[4,10,1,128]{3,2,1,0:T(1,128)S(1)}, u32[]{:S(2)}, u32[]{:S(2)}) %collective-permute-start.18) | collective-permute-done | bytes 20512 | tf_op jit(solution)/shard_map/ppermute | solution.py:32
  182.2 2.4 %collective-permute-start.21 = (f32[4,1,64,128]{3,2,1,0:T(8,128)S(1)}, f32[4,1,64,128]{3,2,1,0:T(8,128)S(1)}, u32[]{:S(2)}, u32[]{:S(2)}) collective-permute-start(f32[4,1,64,128]{3,2,1,0:T(8,128)S(1)} %get-tuple-element.1060), channel_id=1, source_target_pairs={{0,4},{4,8},{8,12},{12,16},{16,20},{20,24},{24,28},{1,5},{5,9},{9,... | collective-permute-start | bytes 393224 | tf_op jit(solution)/shard_map/ppermute | solution.py:31
  185.0 4.4 %collective-permute-done.21 = f32[4,1,64,128]{3,2,1,0:T(8,128)S(1)} collective-permute-done((f32[4,1,64,128]{3,2,1,0:T(8,128)S(1)}, f32[4,1,64,128]{3,2,1,0:T(8,128)S(1)}, u32[]{:S(2)}, u32[]{:S(2)}) %collective-permute-start.21) | collective-permute-done | bytes 131104 | tf_op jit(solution)/shard_map/ppermute | solution.py:31
  192.8 4.2 %collective-permute-done.22 = f32[4,10,1,128]{3,2,1,0:T(1,128)S(1)} collective-permute-done((f32[4,10,1,128]{3,2,1,0:T(1,128)S(1)}, f32[4,10,1,128]{3,2,1,0:T(1,128)S(1)}, u32[]{:S(2)}, u32[]{:S(2)}) %collective-permute-start.22) | collective-permute-done | bytes 20512 | tf_op jit(solution)/shard_map/ppermute | solution.py:32
  (272 shorter events, 111.7 us)
Async XLA Ops:
  2.3 86.7 %collective-permute-start.1 = (f32[4,1,64,128]{3,2,1,0:T(8,128)}, f32[4,1,64,128]{3,2,1,0:T(8,128)S(1)}, u32[]{:S(2)}, u32[]{:S(2)}) collective-permute-start(f32[4,1,64,128]{3,2,1,0:T(8,128)} %get-tuple-element.1101), channel_id=1, source_target_pairs={{0,4},{4,8},{8,12},{12,16},{16,20},{20,24},{24,28},{1,5},{5,9},{9,... | collective-permute-start | bytes 393224 | tf_op jit(solution)/shard_map/ppermute | solution.py:31
  5.8 27.4 %collective-permute-start.24 = (f32[7,256]{1,0:T(8,128)S(1)}, f32[7,256]{1,0:T(8,128)S(1)}, u32[]{:S(2)}, u32[]{:S(2)}) collective-permute-start(f32[7,256]{1,0:T(8,128)S(1)} %get-tuple-element.1111), channel_id=1, source_target_pairs={{0,4},{4,8},{8,12},{12,16},{16,20},{20,24},{24,28},{1,5},{5,9},{9,... | collective-permute-start | bytes 21512 | tf_op jit(solution)/shard_map/ppermute | solution.py:21
  9.3 13.9 %collective-permute-start.32 = (f32[7,256]{1,0:T(8,128)S(1)}, f32[7,256]{1,0:T(8,128)S(1)}, u32[]{:S(2)}, u32[]{:S(2)}) collective-permute-start(f32[7,256]{1,0:T(8,128)S(1)} %get-tuple-element.1106), channel_id=1, source_target_pairs={{0,8},{4,12},{8,16},{12,20},{16,24},{20,28},{1,9},{5,13},{9,17},{1... | collective-permute-start | bytes 21512 | tf_op jit(solution)/shard_map/ppermute | solution.py:21
  11.2 9.3 %collective-permute-start.26 = (f32[7,256]{1,0:T(8,128)S(1)}, f32[7,256]{1,0:T(8,128)S(1)}, u32[]{:S(2)}, u32[]{:S(2)}) collective-permute-start(f32[7,256]{1,0:T(8,128)S(1)} %get-tuple-element.1110), channel_id=1, source_target_pairs={{0,4},{4,8},{8,12},{12,16},{16,20},{20,24},{24,28},{1,5},{5,9},{9,... | collective-permute-start | bytes 21512 | tf_op jit(solution)/shard_map/ppermute | solution.py:21
  13.2 22.3 %collective-permute-start.27 = (f32[7,256]{1,0:T(8,128)S(1)}, f32[7,256]{1,0:T(8,128)S(1)}, u32[]{:S(2)}, u32[]{:S(2)}) collective-permute-start(f32[7,256]{1,0:T(8,128)S(1)} %get-tuple-element.1109), channel_id=1, source_target_pairs={{0,4},{4,8},{8,12},{12,16},{16,20},{20,24},{24,28},{1,5},{5,9},{9,... | collective-permute-start | bytes 21512 | tf_op jit(solution)/shard_map/ppermute | solution.py:21
  20.6 6.5 %collective-permute-start.31 = (f32[7,256]{1,0:T(8,128)S(1)}, f32[7,256]{1,0:T(8,128)S(1)}, u32[]{:S(2)}, u32[]{:S(2)}) collective-permute-start(f32[7,256]{1,0:T(8,128)S(1)} %get-tuple-element.1107), channel_id=1, source_target_pairs={{0,8},{4,12},{8,16},{12,20},{16,24},{20,28},{1,9},{5,13},{9,17},{1... | collective-permute-start | bytes 21512 | tf_op jit(solution)/shard_map/ppermute | solution.py:21
  23.2 13.6 %collective-permute-start.29 = (f32[7,256]{1,0:T(8,128)S(1)}, f32[7,256]{1,0:T(8,128)S(1)}, u32[]{:S(2)}, u32[]{:S(2)}) collective-permute-start(f32[7,256]{1,0:T(8,128)S(1)} %get-tuple-element.1108), channel_id=1, source_target_pairs={{0,8},{4,12},{8,16},{12,20},{16,24},{20,28},{1,9},{5,13},{9,17},{1... | collective-permute-start | bytes 21512 | tf_op jit(solution)/shard_map/ppermute | solution.py:21
  27.1 14.2 %collective-permute-start.33 = (f32[7,256]{1,0:T(8,128)S(1)}, f32[7,256]{1,0:T(8,128)S(1)}, u32[]{:S(2)}, u32[]{:S(2)}) collective-permute-start(f32[7,256]{1,0:T(8,128)S(1)} %collective-permute-done.32), channel_id=1, source_target_pairs={{0,1},{1,2},{2,3},{4,5},{5,6},{6,7},{8,9},{9,10},{10,11},{12,13},{... | collective-permute-start | bytes 21512 | tf_op jit(solution)/shard_map/ppermute | solution.py:21
  33.2 55.9 %collective-permute-start = (f32[4,1,64,128]{3,2,1,0:T(8,128)}, f32[4,1,64,128]{3,2,1,0:T(8,128)}, u32[]{:S(2)}, u32[]{:S(2)}) collective-permute-start(f32[4,1,64,128]{3,2,1,0:T(8,128)} %get-tuple-element.1100), channel_id=1, source_target_pairs={{4,0},{8,4},{12,8},{16,12},{20,16},{24,20},{28,24},{5,1},{9,5},{13... | collective-permute-start | bytes 393224 | tf_op jit(solution)/shard_map/ppermute | solution.py:32
  35.5 8.3 %collective-permute-start.25 = (f32[7,256]{1,0:T(8,128)S(1)}, f32[7,256]{1,0:T(8,128)S(1)}, u32[]{:S(2)}, u32[]{:S(2)}) collective-permute-start(f32[7,256]{1,0:T(8,128)S(1)} %collective-permute-done.24), channel_id=1, source_target_pairs={{1,0},{2,1},{3,2},{5,4},{6,5},{7,6},{9,8},{10,9},{11,10},{13,12},{... | collective-permute-start | bytes 21512 | tf_op jit(solution)/shard_map/ppermute | solution.py:21
  36.8 6.4 %collective-permute-start.28 = (f32[7,256]{1,0:T(8,128)S(1)}, f32[7,256]{1,0:T(8,128)S(1)}, u32[]{:S(2)}, u32[]{:S(2)}) collective-permute-start(f32[7,256]{1,0:T(8,128)S(1)} %collective-permute-done.27), channel_id=1, source_target_pairs={{0,1},{1,2},{2,3},{4,5},{5,6},{6,7},{8,9},{9,10},{10,11},{12,13},{... | collective-permute-start | bytes 21512 | tf_op jit(solution)/shard_map/ppermute | solution.py:21
  41.4 5.5 %collective-permute-start.30 = (f32[7,256]{1,0:T(8,128)S(1)}, f32[7,256]{1,0:T(8,128)S(1)}, u32[]{:S(2)}, u32[]{:S(2)}) collective-permute-start(f32[7,256]{1,0:T(8,128)S(1)} %collective-permute-done.29), channel_id=1, source_target_pairs={{1,0},{2,1},{3,2},{5,4},{6,5},{7,6},{9,8},{10,9},{11,10},{13,12},{... | collective-permute-start | bytes 21512 | tf_op jit(solution)/shard_map/ppermute | solution.py:21
  90.2 8.1 %collective-permute-start.3 = (f32[4,10,1,128]{3,2,1,0:T(1,128)S(1)}, f32[4,10,1,128]{3,2,1,0:T(1,128)S(1)}, u32[]{:S(2)}, u32[]{:S(2)}) collective-permute-start(f32[4,10,1,128]{3,2,1,0:T(1,128)S(1)} %get-tuple-element.1055), channel_id=1, source_target_pairs={{0,1},{1,2},{2,3},{4,5},{5,6},{6,7},{8,9},{9,10},{10,11},{12,13},{... | collective-permute-start | bytes 61448 | tf_op jit(solution)/shard_map/ppermute | solution.py:31
  96.1 5.7 %collective-permute-start.2 = (f32[4,10,1,128]{3,2,1,0:T(1,128)S(1)}, f32[4,10,1,128]{3,2,1,0:T(1,128)S(1)}, u32[]{:S(2)}, u32[]{:S(2)}) collective-permute-start(f32[4,10,1,128]{3,2,1,0:T(1,128)S(1)} %get-tuple-element.1054), channel_id=1, source_target_pairs={{1,0},{2,1},{3,2},{5,4},{6,5},{7,6},{9,8},{10,9},{11,10},{13,12},{... | collective-permute-start | bytes 61448 | tf_op jit(solution)/shard_map/ppermute | solution.py:32
  106.5 7.2 %collective-permute-start.5 = (f32[4,1,64,128]{3,2,1,0:T(8,128)S(1)}, f32[4,1,64,128]{3,2,1,0:T(8,128)S(1)}, u32[]{:S(2)}, u32[]{:S(2)}) collective-permute-start(f32[4,1,64,128]{3,2,1,0:T(8,128)S(1)} %get-tuple-element.1092), channel_id=1, source_target_pairs={{0,4},{4,8},{8,12},{12,16},{16,20},{20,24},{24,28},{1,5},{5,9},{9,... | collective-permute-start | bytes 393224 | tf_op jit(solution)/shard_map/ppermute | solution.py:31
  117.2 5.7 %collective-permute-start.6 = (f32[4,10,1,128]{3,2,1,0:T(1,128)S(1)}, f32[4,10,1,128]{3,2,1,0:T(1,128)S(1)}, u32[]{:S(2)}, u32[]{:S(2)}) collective-permute-start(f32[4,10,1,128]{3,2,1,0:T(1,128)S(1)} %get-tuple-element.1052), channel_id=1, source_target_pairs={{1,0},{2,1},{3,2},{5,4},{6,5},{7,6},{9,8},{10,9},{11,10},{13,12},{... | collective-permute-start | bytes 61448 | tf_op jit(solution)/shard_map/ppermute | solution.py:32
  126.6 7.2 %collective-permute-start.9 = (f32[4,1,64,128]{3,2,1,0:T(8,128)S(1)}, f32[4,1,64,128]{3,2,1,0:T(8,128)S(1)}, u32[]{:S(2)}, u32[]{:S(2)}) collective-permute-start(f32[4,1,64,128]{3,2,1,0:T(8,128)S(1)} %get-tuple-element.1084), channel_id=1, source_target_pairs={{0,4},{4,8},{8,12},{12,16},{16,20},{20,24},{24,28},{1,5},{5,9},{9,... | collective-permute-start | bytes 393224 | tf_op jit(solution)/shard_map/ppermute | solution.py:31
  135.7 5.7 %collective-permute-start.10 = (f32[4,10,1,128]{3,2,1,0:T(1,128)S(1)}, f32[4,10,1,128]{3,2,1,0:T(1,128)S(1)}, u32[]{:S(2)}, u32[]{:S(2)}) collective-permute-start(f32[4,10,1,128]{3,2,1,0:T(1,128)S(1)} %get-tuple-element.1050), channel_id=1, source_target_pairs={{1,0},{2,1},{3,2},{5,4},{6,5},{7,6},{9,8},{10,9},{11,10},{13,12},{... | collective-permute-start | bytes 61448 | tf_op jit(solution)/shard_map/ppermute | solution.py:32
  145.1 7.2 %collective-permute-start.13 = (f32[4,1,64,128]{3,2,1,0:T(8,128)S(1)}, f32[4,1,64,128]{3,2,1,0:T(8,128)S(1)}, u32[]{:S(2)}, u32[]{:S(2)}) collective-permute-start(f32[4,1,64,128]{3,2,1,0:T(8,128)S(1)} %get-tuple-element.1076), channel_id=1, source_target_pairs={{0,4},{4,8},{8,12},{12,16},{16,20},{20,24},{24,28},{1,5},{5,9},{9,... | collective-permute-start | bytes 393224 | tf_op jit(solution)/shard_map/ppermute | solution.py:31
  154.3 5.7 %collective-permute-start.14 = (f32[4,10,1,128]{3,2,1,0:T(1,128)S(1)}, f32[4,10,1,128]{3,2,1,0:T(1,128)S(1)}, u32[]{:S(2)}, u32[]{:S(2)}) collective-permute-start(f32[4,10,1,128]{3,2,1,0:T(1,128)S(1)} %get-tuple-element.1048), channel_id=1, source_target_pairs={{1,0},{2,1},{3,2},{5,4},{6,5},{7,6},{9,8},{10,9},{11,10},{13,12},{... | collective-permute-start | bytes 61448 | tf_op jit(solution)/shard_map/ppermute | solution.py:32
  163.7 7.2 %collective-permute-start.17 = (f32[4,1,64,128]{3,2,1,0:T(8,128)S(1)}, f32[4,1,64,128]{3,2,1,0:T(8,128)S(1)}, u32[]{:S(2)}, u32[]{:S(2)}) collective-permute-start(f32[4,1,64,128]{3,2,1,0:T(8,128)S(1)} %get-tuple-element.1068), channel_id=1, source_target_pairs={{0,4},{4,8},{8,12},{12,16},{16,20},{20,24},{24,28},{1,5},{5,9},{9,... | collective-permute-start | bytes 393224 | tf_op jit(solution)/shard_map/ppermute | solution.py:31
  172.8 5.7 %collective-permute-start.18 = (f32[4,10,1,128]{3,2,1,0:T(1,128)S(1)}, f32[4,10,1,128]{3,2,1,0:T(1,128)S(1)}, u32[]{:S(2)}, u32[]{:S(2)}) collective-permute-start(f32[4,10,1,128]{3,2,1,0:T(1,128)S(1)} %get-tuple-element.1046), channel_id=1, source_target_pairs={{1,0},{2,1},{3,2},{5,4},{6,5},{7,6},{9,8},{10,9},{11,10},{13,12},{... | collective-permute-start | bytes 61448 | tf_op jit(solution)/shard_map/ppermute | solution.py:32
  182.2 7.2 %collective-permute-start.21 = (f32[4,1,64,128]{3,2,1,0:T(8,128)S(1)}, f32[4,1,64,128]{3,2,1,0:T(8,128)S(1)}, u32[]{:S(2)}, u32[]{:S(2)}) collective-permute-start(f32[4,1,64,128]{3,2,1,0:T(8,128)S(1)} %get-tuple-element.1060), channel_id=1, source_target_pairs={{0,4},{4,8},{8,12},{12,16},{16,20},{20,24},{24,28},{1,5},{5,9},{9,... | collective-permute-start | bytes 393224 | tf_op jit(solution)/shard_map/ppermute | solution.py:31
  191.4 5.7 %collective-permute-start.22 = (f32[4,10,1,128]{3,2,1,0:T(1,128)S(1)}, f32[4,10,1,128]{3,2,1,0:T(1,128)S(1)}, u32[]{:S(2)}, u32[]{:S(2)}) collective-permute-start(f32[4,10,1,128]{3,2,1,0:T(1,128)S(1)} %get-tuple-element.1044), channel_id=1, source_target_pairs={{1,0},{2,1},{3,2},{5,4},{6,5},{7,6},{9,8},{10,9},{11,10},{13,12},{... | collective-permute-start | bytes 61448 | tf_op jit(solution)/shard_map/ppermute | solution.py:32
  (59 other events, 335.9 us)
where the time goes:
time: 201 us; the launch traced here: 200 us
  starting transfers between devices  74.6 us (37%)
  waiting for transfers between devices  50.9 us (25%)
  other arithmetic  33.2 us (17%)
  local copies, waits for them, and re-layouts  17.3 us (9%)
  matrix products  17.3 us (9%)
  between operations  5.95 us (3%)
    ppermute x12, starting transfers between devices, with_halo(): before = lax.ppermute(last, axis, up)  31 us
    ppermute x12, waiting for transfers between devices, with_halo(): after = lax.ppermute(leading, axis, down)  24.6 us
    ppermute x10, starting transfers between devices, shifted_2(): return lax.ppermute(x, axis, pairs)  23.8 us
    ppermute x12, waiting for transfers between devices, with_halo(): before = lax.ppermute(last, axis, up)  22.5 us
    ppermute x12, starting transfers between devices, with_halo(): after = lax.ppermute(leading, axis, down)  19.8 us
    dot_general x6, matrix products, ember_update(): jnp.einsum('kxyz,ez->kxye', tile_fields, weight_level, precision=lax.Prec...  11.4 us
    sub x6, other arithmetic, advance(): centre + HORIZONTAL_MIX * spread + VERTICAL_MIX * column_mix  9.19 us
    slice x12, local copies, waits for them, and re-layouts, advance(): lower_level = jnp.concatenate([centre[..., :1], centre[..., :-1]], axis=-1)  8.26 us
  transfers between devices with their start and end apart: 34, of which 18 were waited for; matrix products, arithmetic and copies ran while one was open for 26% of the time, Pallas kernels for 0%

commit v1 on v0

v1 whole, which is shorter than its diff:
```python
import functools

import jax
import jax.numpy as jnp
from jax import lax
from jax.experimental import pallas as pl
from jax.experimental.pallas import tpu as pltpu
from jax.sharding import PartitionSpec as P

STEPS = 6
HORIZONTAL_MIX = 0.1
VERTICAL_MIX = 0.1
ADVECTION = 0.25
DRAG_RATE = 0.6
BURN_RATE = 0.5
HEAT_YIELD = 4.0
DESTINATIONS = ((1, -1), (1, 0), (1, 1), (2, -1), (2, 0), (2, 1))
PAD = 8
CHUNK = 32
MESH = pl.DeviceIdType.MESH


def halves(x):
    high = x.astype(jnp.bfloat16)
    return high, (x - high.astype(jnp.float32)).astype(jnp.bfloat16)


def tent(position, cells):
    centres = lax.broadcasted_iota(jnp.int32, (cells, position.shape[1]), 0).astype(jnp.float32) + 0.5
    return jnp.maximum(0.0, 1.0 - jnp.abs(position - centres))


def kernel(
    nd, nc, fields_ref, embers_ref, counts_ref, advanced_ref, landed_ref,
    state, ysend, yrecv, esend, erecv, split, spread, deposit,
    in_sem, x_send, x_recv, y_send, y_recv, e_send, e_recv,
):
    fields, cx, cy, nz = fields_ref.shape
    slots, capacity = embers_ref.shape[3:]
    d = lax.axis_index("down")
    c = lax.axis_index("cross")
    rows = pl.ds(PAD, cy)

    def inside(a, b):
        return (d + a >= 0) & (d + a < nd) & (c + b >= 0) & (c + b < nc)

    loading = pltpu.make_async_copy(fields_ref, state.at[0, :, pl.ds(1, cx), rows], in_sem)
    loading.start()

    zero_row = jnp.zeros((cy, nz), jnp.float32)
    for b in range(2):
        for k in range(fields):
            state[b, k, 0, PAD:PAD + cy, :] = zero_row
            state[b, k, cx + 1, PAD:PAD + cy, :] = zero_row
    yrecv[...] = jnp.zeros(yrecv.shape, jnp.float32)
    erecv[...] = jnp.zeros(erecv.shape, jnp.float32)

    barrier = pltpu.get_barrier_semaphore()
    peers = [(a, b) for a in (-2, -1, 1, 2) for b in (-1, 0, 1)] + [(0, -1), (0, 1)]
    present = 0
    for a, b in peers:
        there = inside(a, b)
        present = present + there.astype(jnp.int32)

        @pl.when(there)
        def _(a=a, b=b):
            pl.semaphore_signal(barrier, inc=1, device_id=(d + a, c + b), device_id_type=MESH)

    lane = lax.broadcasted_iota(jnp.int32, (1, capacity), 1)
    for j in range(slots):
        live = lane < counts_ref[0, 0, j]
        for i in range(7):
            esend[j, i:i + 1, :] = jnp.where(live, embers_ref[i, 0, 0, j:j + 1, :], 0.0)
        esend[j, 7:8, :] = jnp.zeros((1, capacity), jnp.float32)

    def x_copy(b, side):
        source, target, by = ((cx, 0, 1), (1, cx + 1, -1))[side]
        return pltpu.make_async_remote_copy(
            src_ref=state.at[b, :, source, rows],
            dst_ref=state.at[b, :, target, rows],
            send_sem=x_send.at[b, side], recv_sem=x_recv.at[b, side],
            device_id=(d + by, c), device_id_type=MESH,
        )

    def y_copy(b, side):
        by = (1, -1)[side]
        return pltpu.make_async_remote_copy(
            src_ref=ysend.at[b, side], dst_ref=yrecv.at[b, side],
            send_sem=y_send.at[b, side], recv_sem=y_recv.at[b, side],
            device_id=(d, c + by), device_id_type=MESH,
        )

    def e_copy(j):
        a, b = DESTINATIONS[j]
        return pltpu.make_async_remote_copy(
            src_ref=esend.at[j], dst_ref=erecv.at[j],
            send_sem=e_send.at[j], recv_sem=e_recv.at[j],
            device_id=(d + a, c + b), device_id_type=MESH,
        )

    def start_x(b):
        for side, by in enumerate((1, -1)):
            @pl.when(inside(by, 0))
            def _(side=side):
                x_copy(b, side).start()

    def wait_x(b):
        for side, by in enumerate((1, -1)):
            @pl.when(inside(-by, 0))
            def _(side=side):
                x_copy(b, side).wait_recv()

            @pl.when(inside(by, 0))
            def _(side=side):
                x_copy(b, side).wait_send()

    def start_y(b):
        for k in range(fields):
            for i in range(cx):
                ysend[b, 0, k, i:i + 1, :] = state[b, k, i + 1, PAD + cy - 1:PAD + cy, :]
                ysend[b, 1, k, i:i + 1, :] = state[b, k, i + 1, PAD:PAD + 1, :]
        for side, by in enumerate((1, -1)):
            @pl.when(inside(0, by))
            def _(side=side):
                y_copy(b, side).start()

    def wait_y(b):
        for side, by in enumerate((1, -1)):
            @pl.when(inside(0, -by))
            def _(side=side):
                y_copy(b, side).wait_recv()

            @pl.when(inside(0, by))
            def _(side=side):
                y_copy(b, side).wait_send()

        for k in range(fields):
            for i in range(cx):
                state[b, k, i + 1, PAD - 1:PAD, :] = yrecv[b, 0, k, i:i + 1, :]
                state[b, k, i + 1, PAD + cy:PAD + cy + 1, :] = yrecv[b, 1, k, i:i + 1, :]

    level = lax.broadcasted_iota(jnp.int32, (CHUNK, nz), 1)
    keep = 1.0 - 4.0 * HORIZONTAL_MIX - 2.0 * VERTICAL_MIX

    def stencil(b, i, last):
        for y in range(0, cy, CHUNK):
            here = slice(PAD + y, PAD + y + CHUNK)
            u = state[b, 0, i, here, :] * (0.5 * ADVECTION)
            v = state[b, 1, i, here, :] * (0.5 * ADVECTION)
            for k in range(fields):
                centre = state[b, k, i, here, :]
                eastern = state[b, k, i + 1, here, :]
                western = state[b, k, i - 1, here, :]
                northern = state[b, k, i, PAD + y + 1:PAD + y + 1 + CHUNK, :]
                southern = state[b, k, i, PAD + y - 1:PAD + y - 1 + CHUNK, :]
                upper = jnp.where(level == nz - 1, centre, pltpu.roll(centre, nz - 1, 1))
                lower = jnp.where(level == 0, centre, pltpu.roll(centre, 1, 1))
                new = (
                    keep * centre
                    + HORIZONTAL_MIX * ((eastern + western) + (northern + southern))
                    + VERTICAL_MIX * (upper + lower)
                    - (u * (eastern - western) + v * (northern - southern))
                )
                if not last:
                    state[1 - b, k, i, here, :] = new
                else:
                    if k == 2:
                        new = new + deposit[pl.ds(pl.multiple_of((i - 1) * cy + y, CHUNK), CHUNK), :]
                    advanced_ref[k, i - 1, y:y + CHUNK, :] = new

    def embers_of(j):
        a, b = DESTINATIONS[j]

        @pl.when(inside(-a, -b))
        def _():
            e_copy(j).wait_recv()

        @pl.when(inside(a, b))
        def _():
            e_copy(j).wait_send()

        def part(i):
            return erecv[j, i:i + 1, :]

        wx = tent(part(0) * cx, cx)
        wy = tent(part(1) * cy, cy)
        wz = tent(part(2) * nz, nz)
        z_high, z_low = halves(wz)
        z_both = jnp.concatenate([z_high, z_high], axis=0)
        for i in range(cx):
            at = slice(i * cy, (i + 1) * cy)
            spread[0, at, :], spread[1, at, :] = halves(wx[i:i + 1, :] * wy)
        sampled = []
        for k in range(fields):
            of = split[k * cx * cy:(k + 1) * cx * cy, :]
            column = jnp.dot(of, z_both, preferred_element_type=jnp.float32)
            column += jnp.dot(of[:, :nz], z_low, preferred_element_type=jnp.float32)
            across = jnp.sum(column.reshape(cx, cy, capacity) * wy[None], axis=1)
            sampled.append(jnp.sum(across * wx, axis=0, keepdims=True))
        ue, ve, mass, heat = part(3), part(4), part(5), part(6)
        burned = mass * BURN_RATE * jax.nn.sigmoid(heat + sampled[2] - sampled[3])
        living = mass > 0.0
        outs = (
            ue + DRAG_RATE * (sampled[0] - ue),
            ve + DRAG_RATE * (sampled[1] - ve),
            heat + DRAG_RATE * (sampled[2] - heat),
            mass - burned,
        )
        for i in range(4):
            landed_ref[i, 0, 0, j:j + 1, :] = jnp.where(living, outs[i], 0.0)
        g_high, g_low = halves(wz * (HEAT_YIELD * burned))

        def nt(p, q):
            return lax.dot_general(p, q, (((1,), (1,)), ((), ())), preferred_element_type=jnp.float32)

        s_high = spread[0]
        add = nt(s_high, g_high) + nt(s_high, g_low) + nt(spread[1], g_high)
        deposit[...] = add if j == 0 else deposit[...] + add

    pl.semaphore_wait(barrier, present)
    for j in range(slots):
        @pl.when(inside(*DESTINATIONS[j]))
        def _(j=j):
            e_copy(j).start()
    loading.wait()

    for step in range(STEPS):
        b = step % 2
        start_x(b)
        start_y(b)
        if step == 0:
            for k in range(fields):
                for i in range(cx):
                    at = slice((k * cx + i) * cy, (k * cx + i + 1) * cy)
                    split[at, :nz], split[at, nz:] = halves(state[0, k, i + 1, PAD:PAD + cy, :])
        embers_of(step)
        wait_y(b)
        last = step == STEPS - 1

        def inner(i, carry, b=b, last=last):
            stencil(b, i, last)
            return carry

        lax.fori_loop(2, cx, inner, 0)
        wait_x(b)
        stencil(b, 1, last)
        stencil(b, cx, last)


def solution(mesh):
    nd, nc = mesh.shape["down"], mesh.shape["cross"]

    def local(fields, embers, counts):
        k, cx, cy, nz = fields.shape
        slots, capacity = embers.shape[3:]
        sem = pltpu.SemaphoreType.DMA
        return pl.pallas_call(
            functools.partial(kernel, nd, nc),
            out_shape=(
                jax.ShapeDtypeStruct(fields.shape, jnp.float32),
                jax.ShapeDtypeStruct((4, 1, 1, slots, capacity), jnp.float32),
            ),
            in_specs=[
                pl.BlockSpec(memory_space=pl.ANY),
                pl.BlockSpec(memory_space=pltpu.VMEM),
                pl.BlockSpec(memory_space=pltpu.SMEM),
            ],
            out_specs=[pl.BlockSpec(memory_space=pltpu.VMEM)] * 2,
            scratch_shapes=[
                pltpu.VMEM((2, k, cx + 2, cy + 2 * PAD, nz), jnp.float32),
                pltpu.VMEM((2, 2, k, cx, nz), jnp.float32),
                pltpu.VMEM((2, 2, k, cx, nz), jnp.float32),
                pltpu.VMEM((slots, 8, capacity), jnp.float32),
                pltpu.VMEM((slots, 8, capacity), jnp.float32),
                pltpu.VMEM((k * cx * cy, 2 * nz), jnp.bfloat16),
                pltpu.VMEM((2, cx * cy, capacity), jnp.bfloat16),
                pltpu.VMEM((cx * cy, nz), jnp.float32),
                sem, sem((2, 2)), sem((2, 2)), sem((2, 2)), sem((2, 2)),
                sem((slots,)), sem((slots,)),
            ],
            compiler_params=pltpu.CompilerParams(
                collective_id=0, has_side_effects=True, vmem_limit_bytes=40 * 1024 * 1024
            ),
            name="fire_step",
        )(fields, embers, counts)

    placed = (
        P(None, "down", "cross", None),
        P(None, "down", "cross", None, None),
        P("down", "cross", None),
    )
    return jax.shard_map(
        local,
        mesh=mesh,
        in_specs=placed,
        out_specs=(P(None, "down", "cross", None), P(None, "down", "cross", None, None)),
        check_vma=False,
    )
```

time: 201 us -> 37 us (0.18)
  the two profiles are of different devices: /device:TPU:4 before, /device:TPU:3 now
where the time goes in v1:
time: 37 us; the launch traced here: 36.8 us
  Pallas kernels  32.5 us (88%)
  local copies, waits for them, and re-layouts  3.62 us (10%)
  between operations  0.66 us (2%)
    pallas_call x1, Pallas kernels, local(): pl.pallas_call(functools.partial(kernel, nd, nc), out_shape=(jax.ShapeDty...  32.5 us
    unnamed x6, local copies, waits for them, and re-layouts  2.99 us

profile of v1, /device:TPU:3, one launch (start us, length us, event | category | flops | bytes accessed | tf_op | source)
XLA Modules:
  0.0 36.8 jit_solution(2830515433313681027)
XLA Ops:
  0.6 0.0 copy-start.1
  0.6 0.8 %copy.5.embers_ref = f32[7,1,1,6,256]{4,3,2,1,0:T(8,128)S(1)} copy(f32[7,1,1,6,256]{4,2,3,1,0:T(1,128)} %param.4) | data formatting | bytes 86016 | tf_op args[1]
  1.4 0.0 copy-done.1
  1.4 0.0 copy-start
  1.5 1.2 %copy-done = f32[4,8,64,128]{3,2,1,0:T(8,128)S(1)} copy-done((f32[4,8,64,128]{3,2,1,0:T(8,128)S(1)}, f32[4,8,64,128]{3,2,1,0:T(8,128)}, u32[]{:S(2)}) %copy-start) | copy-done | bytes 1048600
  2.7 32.5 %fire_step.1 = (f32[4,8,64,128]{3,2,1,0:T(8,128)S(1)}, f32[4,1,1,6,256]{4,3,2,1,0:T(8,128)S(1)}) custom-call(f32[4,8,64,128]{3,2,1,0:T(8,128)S(1)} %copy-done, f32[7,1,1,6,256]{4,3,2,1,0:T(8,128)S(1)} %copy.5.embers_ref, s32[1,1,6]{2,1,0:T(1,128)S(1)} %copy-done.1), custom_call_target="tpu_custom_call" | custom-call | tf_op jit(solution)/shard_map/fire_step/pallas_call | solution.py:257
  35.2 0.6 %copy.6 = f32[4,1,1,6,256]{4,2,3,1,0:T(1,128)} copy(f32[4,1,1,6,256]{4,3,2,1,0:T(8,128)S(1)} %get-tuple-element.3) | data formatting | bytes 49152 | tf_op jit(solution)/shard_map/fire_step/pallas_call | solution.py:257
  35.9 1.0 %copy.8 = f32[4,8,64,128]{3,2,1,0:T(8,128)} copy(f32[4,8,64,128]{3,2,1,0:T(8,128)S(1)} %get-tuple-element.6) | data formatting | bytes 2097152
Async XLA Ops:
  0.6 0.8 %copy-start.1 = (s32[1,1,6]{2,1,0:T(1,128)S(1)}, s32[1,1,6]{2,1,0:T(1,128)}, u32[]{:S(2)}) copy-start(s32[1,1,6]{2,1,0:T(1,128)} %counts_ref.1) | copy-start | bytes 76
  1.4 1.2 %copy-start = (f32[4,8,64,128]{3,2,1,0:T(8,128)S(1)}, f32[4,8,64,128]{3,2,1,0:T(8,128)}, u32[]{:S(2)}) copy-start(f32[4,8,64,128]{3,2,1,0:T(8,128)} %fields_ref.1) | copy-start | bytes 3145732

commit v2 on v1

--- a/solution.py
+++ b/solution.py
@@ -36,10 +36,11 @@
     in_sem, x_send, x_recv, y_send, y_recv, e_send, e_recv,
 ):
     fields, cx, cy, nz = fields_ref.shape
-    slots, capacity = embers_ref.shape[3:]
+    slots, capacity = len(DESTINATIONS), embers_ref.shape[2]
     d = lax.axis_index("down")
     c = lax.axis_index("cross")
     rows = pl.ds(PAD, cy)
+    parts = cy // CHUNK
 
     def inside(a, b):
         return (d + a >= 0) & (d + a < nd) & (c + b >= 0) & (c + b < nc)
@@ -70,15 +71,16 @@
     for j in range(slots):
         live = lane < counts_ref[0, 0, j]
         for i in range(7):
-            esend[j, i:i + 1, :] = jnp.where(live, embers_ref[i, 0, 0, j:j + 1, :], 0.0)
+            esend[j, i:i + 1, :] = jnp.where(live, embers_ref[i * slots + j], 0.0)
         esend[j, 7:8, :] = jnp.zeros((1, capacity), jnp.float32)
 
-    def x_copy(b, side):
+    def x_copy(b, side, part):
         source, target, by = ((cx, 0, 1), (1, cx + 1, -1))[side]
+        band = pl.ds(PAD + part * CHUNK, CHUNK)
         return pltpu.make_async_remote_copy(
-            src_ref=state.at[b, :, source, rows],
-            dst_ref=state.at[b, :, target, rows],
-            send_sem=x_send.at[b, side], recv_sem=x_recv.at[b, side],
+            src_ref=state.at[b, :, source, band],
+            dst_ref=state.at[b, :, target, band],
+            send_sem=x_send.at[b, side, part], recv_sem=x_recv.at[b, side, part],
             device_id=(d + by, c), device_id_type=MESH,
         )
 
@@ -98,42 +100,35 @@
             device_id=(d + a, c + b), device_id_type=MESH,
         )
 
-    def start_x(b):
+    def each_side(down, from_there, act):
         for side, by in enumerate((1, -1)):
-            @pl.when(inside(by, 0))
+            by = -by if from_there else by
+
+            @pl.when(inside(by, 0) if down else inside(0, by))
             def _(side=side):
-                x_copy(b, side).start()
-
-    def wait_x(b):
-        for side, by in enumerate((1, -1)):
-            @pl.when(inside(-by, 0))
-            def _(side=side):
-                x_copy(b, side).wait_recv()
-
-            @pl.when(inside(by, 0))
-            def _(side=side):
-                x_copy(b, side).wait_send()
+                act(side)
+
+    def start_x(b, part):
+        each_side(True, False, lambda side: x_copy(b, side, part).start())
+
+    def arrive_x(b, part):
+        each_side(True, True, lambda side: x_copy(b, side, part).wait_recv())
+
+    def sent_x(b, part):
+        each_side(True, False, lambda side: x_copy(b, side, part).wait_send())
+
+    def sent_y(b):
+        each_side(False, False, lambda side: y_copy(b, side).wait_send())
 
     def start_y(b):
         for k in range(fields):
             for i in range(cx):
                 ysend[b, 0, k, i:i + 1, :] = state[b, k, i + 1, PAD + cy - 1:PAD + cy, :]
                 ysend[b, 1, k, i:i + 1, :] = state[b, k, i + 1, PAD:PAD + 1, :]
-        for side, by in enumerate((1, -1)):
-            @pl.when(inside(0, by))
-            def _(side=side):
-                y_copy(b, side).start()
-
-    def wait_y(b):
-        for side, by in enumerate((1, -1)):
-            @pl.when(inside(0, -by))
-            def _(side=side):
-                y_copy(b, side).wait_recv()
-
-            @pl.when(inside(0, by))
-            def _(side=side):
-                y_copy(b, side).wait_send()
-
+        each_side(False, False, lambda side: y_copy(b, side).start())
+
+    def arrive_y(b):
+        each_side(False, True, lambda side: y_copy(b, side).wait_recv())
         for k in range(fields):
             for i in range(cx):
                 state[b, k, i + 1, PAD - 1:PAD, :] = yrecv[b, 0, k, i:i + 1, :]
@@ -142,8 +137,8 @@
     level = lax.broadcasted_iota(jnp.int32, (CHUNK, nz), 1)
     keep = 1.0 - 4.0 * HORIZONTAL_MIX - 2.0 * VERTICAL_MIX
 
-    def stencil(b, i, last):
-        for y in range(0, cy, CHUNK):
+    def stencil(b, i, part, last):
+        for y in (part * CHUNK,):
             here = slice(PAD + y, PAD + y + CHUNK)
             u = state[b, 0, i, here, :] * (0.5 * ADVECTION)
             v = state[b, 1, i, here, :] * (0.5 * ADVECTION)
@@ -174,10 +169,6 @@
         @pl.when(inside(-a, -b))
         def _():
             e_copy(j).wait_recv()
-
-        @pl.when(inside(a, b))
-        def _():
-            e_copy(j).wait_send()
 
         def part(i):
             return erecv[j, i:i + 1, :]
@@ -207,7 +198,7 @@
             mass - burned,
         )
         for i in range(4):
-            landed_ref[i, 0, 0, j:j + 1, :] = jnp.where(living, outs[i], 0.0)
+            landed_ref[i * slots + j] = jnp.where(living, outs[i], 0.0)
         g_high, g_low = halves(wz * (HEAT_YIELD * burned))
 
         def nt(p, q):
@@ -224,27 +215,45 @@
             e_copy(j).start()
     loading.wait()
 
+    for part in range(parts):
+        start_x(0, part)
+    start_y(0)
+    for k in range(fields):
+        for i in range(cx):
+            at = slice((k * cx + i) * cy, (k * cx + i + 1) * cy)
+            split[at, :nz], split[at, nz:] = halves(state[0, k, i + 1, PAD:PAD + cy, :])
+
     for step in range(STEPS):
         b = step % 2
-        start_x(b)
-        start_y(b)
-        if step == 0:
-            for k in range(fields):
-                for i in range(cx):
-                    at = slice((k * cx + i) * cy, (k * cx + i + 1) * cy)
-                    split[at, :nz], split[at, nz:] = halves(state[0, k, i + 1, PAD:PAD + cy, :])
+        last = step == STEPS - 1
         embers_of(step)
-        wait_y(b)
-        last = step == STEPS - 1
-
-        def inner(i, carry, b=b, last=last):
-            stencil(b, i, last)
-            return carry
-
-        lax.fori_loop(2, cx, inner, 0)
-        wait_x(b)
-        stencil(b, 1, last)
-        stencil(b, cx, last)
+        arrive_y(b)
+        for part in range(parts):
+            arrive_x(b, part)
+            if step > 0:
+                sent_x(1 - b, part)
+            stencil(b, 1, part, last)
+            stencil(b, cx, part, last)
+            if not last:
+                start_x(1 - b, part)
+            if part == 0:
+                def inner(i, carry, b=b, last=last):
+                    for part in range(parts):
+                        stencil(b, i, part, last)
+                    return carry
+
+                lax.fori_loop(2, cx, inner, 0)
+        if step > 0:
+            sent_y(1 - b)
+        if not last:
+            start_y(1 - b)
+    for part in range(parts):
+        sent_x((STEPS - 1) % 2, part)
+    sent_y((STEPS - 1) % 2)
+    for j in range(slots):
+        @pl.when(inside(*DESTINATIONS[j]))
+        def _(j=j):
+            e_copy(j).wait_send()
 
 
 def solution(mesh):
@@ -254,14 +263,14 @@
         k, cx, cy, nz = fields.shape
         slots, capacity = embers.shape[3:]
         sem = pltpu.SemaphoreType.DMA
-        return pl.pallas_call(
+        advanced, landed = pl.pallas_call(
             functools.partial(kernel, nd, nc),
             out_shape=(
                 jax.ShapeDtypeStruct(fields.shape, jnp.float32),
-                jax.ShapeDtypeStruct((4, 1, 1, slots, capacity), jnp.float32),
+                jax.ShapeDtypeStruct((4 * slots, 1, capacity), jnp.float32),
             ),
             in_specs=[
-                pl.BlockSpec(memory_space=pl.ANY),
+                pl.BlockSpec(memory_space=pltpu.HBM),
                 pl.BlockSpec(memory_space=pltpu.VMEM),
                 pl.BlockSpec(memory_space=pltpu.SMEM),
             ],
@@ -275,14 +284,15 @@
                 pltpu.VMEM((k * cx * cy, 2 * nz), jnp.bfloat16),
                 pltpu.VMEM((2, cx * cy, capacity), jnp.bfloat16),
                 pltpu.VMEM((cx * cy, nz), jnp.float32),
-                sem, sem((2, 2)), sem((2, 2)), sem((2, 2)), sem((2, 2)),
+                sem, sem((2, 2, cy // CHUNK)), sem((2, 2, cy // CHUNK)), sem((2, 2)), sem((2, 2)),
                 sem((slots,)), sem((slots,)),
             ],
             compiler_params=pltpu.CompilerParams(
                 collective_id=0, has_side_effects=True, vmem_limit_bytes=40 * 1024 * 1024
             ),
             name="fire_step",
-        )(fields, embers, counts)
+        )(fields, embers.reshape(7 * slots, 1, capacity), counts)
+        return advanced, landed.reshape(4, 1, 1, slots, capacity)
 
     placed = (
         P(None, "down", "cross", None),

time: 37 us -> 35.7 us (0.965)
  Pallas kernels: 32.5 us -> 30.6 us
  local copies, waits for them, and re-layouts: 3.62 us -> 4.24 us
    pallas_call x1, Pallas kernels: 32.5 us -> 30.6 us  [local(): pl.pallas_call(functools.partial(kernel, nd, nc), out_shape=(jax.ShapeDty...]
    unnamed x6 -> x8, local copies, waits for them, and re-layouts: 2.99 us -> 4.24 us
    pallas_call x1 -> x0, local copies, waits for them, and re-layouts: 0.63 us -> none  [local(): pl.pallas_call(functools.partial(kernel, nd, nc), out_shape=(jax.ShapeDty...]
where the time goes in v2:
time: 35.7 us; the launch traced here: 35.5 us
  Pallas kernels  30.6 us (86%)
  local copies, waits for them, and re-layouts  4.24 us (12%)
  between operations  0.65 us (2%)
    pallas_call x1, Pallas kernels, local(): pl.pallas_call(functools.partial(kernel, nd, nc), out_shape=(jax.ShapeDty...  30.6 us
    unnamed x8, local copies, waits for them, and re-layouts  4.24 us

profile of v2, /device:TPU:3, one launch (start us, length us, event | category | flops | bytes accessed | tf_op | source)
XLA Modules:
  0.0 35.5 jit_solution(16107749071804350577)
XLA Ops:
  0.6 0.0 copy-start.2
  0.6 0.6 %copy-done.2 = s32[1,1,6]{2,1,0:T(1,128)S(1)} copy-done((s32[1,1,6]{2,1,0:T(1,128)S(1)}, s32[1,1,6]{2,1,0:T(1,128)}, u32[]{:S(2)}) %copy-start.2) | copy-done | bytes 48
  1.3 0.0 copy-start
  1.3 1.2 %copy-done = f32[4,8,64,128]{3,2,1,0:T(8,128)S(1)} copy-done((f32[4,8,64,128]{3,2,1,0:T(8,128)S(1)}, f32[4,8,64,128]{3,2,1,0:T(8,128)}, u32[]{:S(2)}) %copy-start) | copy-done | bytes 1048600
  2.5 0.0 copy-start.1
  2.5 0.8 %copy-done.1 = f32[7,1,1,6,256]{4,2,3,1,0:T(1,128)S(1)} copy-done((f32[7,1,1,6,256]{4,2,3,1,0:T(1,128)S(1)}, f32[7,1,1,6,256]{4,2,3,1,0:T(1,128)}, u32[]{:S(2)}) %copy-start.1) | copy-done | bytes 43032
  3.3 30.6 %fire_step.1 = (f32[4,8,64,128]{3,2,1,0:T(8,128)S(1)}, f32[24,1,256]{2,1,0:T(1,128)S(1)}) custom-call(f32[4,8,64,128]{3,2,1,0:T(8,128)S(1)} %copy-done, f32[42,1,256]{2,1,0:T(1,128)S(1)} %bitcast.4, s32[1,1,6]{2,1,0:T(1,128)S(1)} %copy-done.2), custom_call_target="tpu_custom_call" | custom-call | tf_op jit(solution)/shard_map/fire_step/pallas_call | solution.py:266
  33.9 1.0 %copy.8 = f32[4,8,64,128]{3,2,1,0:T(8,128)} copy(f32[4,8,64,128]{3,2,1,0:T(8,128)S(1)} %get-tuple-element.10) | data formatting | bytes 2097152
  34.9 0.6 %copy.9 = f32[4,1,1,6,256]{4,2,3,1,0:T(1,128)} copy(f32[4,1,1,6,256]{4,2,3,1,0:T(1,128)S(1)} %bitcast.5) | data formatting | bytes 49152
Async XLA Ops:
  0.6 0.7 %copy-start.2 = (s32[1,1,6]{2,1,0:T(1,128)S(1)}, s32[1,1,6]{2,1,0:T(1,128)}, u32[]{:S(2)}) copy-start(s32[1,1,6]{2,1,0:T(1,128)} %counts_ref.1) | copy-start | bytes 76
  1.3 1.2 %copy-start = (f32[4,8,64,128]{3,2,1,0:T(8,128)S(1)}, f32[4,8,64,128]{3,2,1,0:T(8,128)}, u32[]{:S(2)}) copy-start(f32[4,8,64,128]{3,2,1,0:T(8,128)} %fields_ref.1) | copy-start | bytes 3145732
  2.5 0.8 %copy-start.1 = (f32[7,1,1,6,256]{4,2,3,1,0:T(1,128)S(1)}, f32[7,1,1,6,256]{4,2,3,1,0:T(1,128)}, u32[]{:S(2)}) copy-start(f32[7,1,1,6,256]{4,2,3,1,0:T(1,128)} %param.4) | copy-start | bytes 129028

commit v3 on v2

--- a/solution.py
+++ b/solution.py
@@ -32,8 +32,8 @@
 
 def kernel(
     nd, nc, fields_ref, embers_ref, counts_ref, advanced_ref, landed_ref,
-    state, ysend, yrecv, esend, erecv, split, spread, deposit,
-    in_sem, x_send, x_recv, y_send, y_recv, e_send, e_recv,
+    state, ysend, yrecv, esend, erecv, split, spread, deposit, result,
+    in_sem, out_sem, edge_sem, x_send, x_recv, y_send, y_recv, e_send, e_recv,
 ):
     fields, cx, cy, nz = fields_ref.shape
     slots, capacity = len(DESTINATIONS), embers_ref.shape[2]
@@ -41,6 +41,7 @@
     c = lax.axis_index("cross")
     rows = pl.ds(PAD, cy)
     parts = cy // CHUNK
+    cells = cx * cy
 
     def inside(a, b):
         return (d + a >= 0) & (d + a < nd) & (c + b >= 0) & (c + b < nc)
@@ -161,7 +162,7 @@
                 else:
                     if k == 2:
                         new = new + deposit[pl.ds(pl.multiple_of((i - 1) * cy + y, CHUNK), CHUNK), :]
-                    advanced_ref[k, i - 1, y:y + CHUNK, :] = new
+                    result[k, i - 1, y:y + CHUNK, :] = new
 
     def embers_of(j):
         a, b = DESTINATIONS[j]
@@ -176,18 +177,14 @@
         wx = tent(part(0) * cx, cx)
         wy = tent(part(1) * cy, cy)
         wz = tent(part(2) * nz, nz)
-        z_high, z_low = halves(wz)
-        z_both = jnp.concatenate([z_high, z_high], axis=0)
         for i in range(cx):
-            at = slice(i * cy, (i + 1) * cy)
-            spread[0, at, :], spread[1, at, :] = halves(wx[i:i + 1, :] * wy)
-        sampled = []
-        for k in range(fields):
-            of = split[k * cx * cy:(k + 1) * cx * cy, :]
-            column = jnp.dot(of, z_both, preferred_element_type=jnp.float32)
-            column += jnp.dot(of[:, :nz], z_low, preferred_element_type=jnp.float32)
-            across = jnp.sum(column.reshape(cx, cy, capacity) * wy[None], axis=1)
-            sampled.append(jnp.sum(across * wx, axis=0, keepdims=True))
+            high, low = halves(wx[i:i + 1, :] * wy)
+            spread[i * cy:(i + 1) * cy, :] = high
+            spread[cells + i * cy:cells + (i + 1) * cy, :] = low
+            spread[2 * cells + i * cy:2 * cells + (i + 1) * cy, :] = high
+        columns = jnp.dot(split[...], spread[...], preferred_element_type=jnp.float32)
+        weighed = jnp.sum(columns.reshape(fields, nz, capacity) * wz[None], axis=1)
+        sampled = [weighed[k:k + 1, :] for k in range(fields)]
         ue, ve, mass, heat = part(3), part(4), part(5), part(6)
         burned = mass * BURN_RATE * jax.nn.sigmoid(heat + sampled[2] - sampled[3])
         living = mass > 0.0
@@ -204,8 +201,8 @@
         def nt(p, q):
             return lax.dot_general(p, q, (((1,), (1,)), ((), ())), preferred_element_type=jnp.float32)
 
-        s_high = spread[0]
-        add = nt(s_high, g_high) + nt(s_high, g_low) + nt(spread[1], g_high)
+        both = nt(spread[:cells, :], jnp.concatenate([g_high, g_low], axis=0))
+        add = both[:, :nz] + both[:, nz:] + nt(spread[cells:2 * cells, :], g_high)
         deposit[...] = add if j == 0 else deposit[...] + add
 
     pl.semaphore_wait(barrier, present)
@@ -219,10 +216,15 @@
         start_x(0, part)
     start_y(0)
     for k in range(fields):
-        for i in range(cx):
-            at = slice((k * cx + i) * cy, (k * cx + i + 1) * cy)
-            split[at, :nz], split[at, nz:] = halves(state[0, k, i + 1, PAD:PAD + cy, :])
-
+        at = slice(k * nz, (k + 1) * nz)
+        own = state[0, k, 1:cx + 1, PAD:PAD + cy, :].reshape(cells, nz)
+        high, low = halves(own.T)
+        split[at, :cells] = high
+        split[at, cells:2 * cells] = high
+        split[at, 2 * cells:] = low
+
+    inner_rows = pl.ds(1, cx - 2)
+    inner_out = pltpu.make_async_copy(result.at[:, inner_rows], advanced_ref.at[:, inner_rows], out_sem.at[0])
     for step in range(STEPS):
         b = step % 2
         last = step == STEPS - 1
@@ -243,10 +245,16 @@
                     return carry
 
                 lax.fori_loop(2, cx, inner, 0)
+                if last:
+                    inner_out.start()
         if step > 0:
             sent_y(1 - b)
         if not last:
             start_y(1 - b)
+    outer_out = []
+    for side, i in enumerate((0, cx - 1)):
+        outer_out.append(pltpu.make_async_copy(result.at[:, i], advanced_ref.at[:, i], edge_sem.at[side]))
+        outer_out[side].start()
     for part in range(parts):
         sent_x((STEPS - 1) % 2, part)
     sent_y((STEPS - 1) % 2)
@@ -255,6 +263,9 @@
         def _(j=j):
             e_copy(j).wait_send()
 
+    inner_out.wait()
+    for copy in outer_out:
+        copy.wait()
 
 def solution(mesh):
     nd, nc = mesh.shape["down"], mesh.shape["cross"]
@@ -274,21 +285,22 @@
                 pl.BlockSpec(memory_space=pltpu.VMEM),
                 pl.BlockSpec(memory_space=pltpu.SMEM),
             ],
-            out_specs=[pl.BlockSpec(memory_space=pltpu.VMEM)] * 2,
+            out_specs=[pl.BlockSpec(memory_space=pltpu.HBM), pl.BlockSpec(memory_space=pltpu.VMEM)],
             scratch_shapes=[
                 pltpu.VMEM((2, k, cx + 2, cy + 2 * PAD, nz), jnp.float32),
                 pltpu.VMEM((2, 2, k, cx, nz), jnp.float32),
                 pltpu.VMEM((2, 2, k, cx, nz), jnp.float32),
                 pltpu.VMEM((slots, 8, capacity), jnp.float32),
                 pltpu.VMEM((slots, 8, capacity), jnp.float32),
-                pltpu.VMEM((k * cx * cy, 2 * nz), jnp.bfloat16),
-                pltpu.VMEM((2, cx * cy, capacity), jnp.bfloat16),
+                pltpu.VMEM((k * nz, 3 * cx * cy), jnp.bfloat16),
+                pltpu.VMEM((3 * cx * cy, capacity), jnp.bfloat16),
                 pltpu.VMEM((cx * cy, nz), jnp.float32),
-                sem, sem((2, 2, cy // CHUNK)), sem((2, 2, cy // CHUNK)), sem((2, 2)), sem((2, 2)),
+                pltpu.VMEM(fields.shape, jnp.float32),
+                sem, sem((1,)), sem((2,)), sem((2, 2, cy // CHUNK)), sem((2, 2, cy // CHUNK)), sem((2, 2)), sem((2, 2)),
                 sem((slots,)), sem((slots,)),
             ],
             compiler_params=pltpu.CompilerParams(
-                collective_id=0, has_side_effects=True, vmem_limit_bytes=40 * 1024 * 1024
+                collective_id=0, has_side_effects=True, vmem_limit_bytes=60 * 1024 * 1024
             ),
             name="fire_step",
         )(fields, embers.reshape(7 * slots, 1, capacity), counts)

time: 35.7 us -> 36 us (level)
  Pallas kernels: 30.6 us -> 32.2 us
  local copies, waits for them, and re-layouts: 4.24 us -> 2.92 us
    pallas_call x1, Pallas kernels: 30.6 us -> 32.2 us  [local(): pl.pallas_call(functools.partial(kernel, nd, nc), out_shape=(jax.ShapeDty...]
    unnamed x8 -> x4, local copies, waits for them, and re-layouts: 4.24 us -> 2.92 us
where the time goes in v3:
time: 36 us; the launch traced here: 35.8 us
  Pallas kernels  32.2 us (89%)
  local copies, waits for them, and re-layouts  2.92 us (8%)
  between operations  0.65 us (2%)
    pallas_call x1, Pallas kernels, local(): pl.pallas_call(functools.partial(kernel, nd, nc), out_shape=(jax.ShapeDty...  32.2 us
    unnamed x4, local copies, waits for them, and re-layouts  2.92 us

profile of v3, /device:TPU:3, one launch (start us, length us, event | category | flops | bytes accessed | tf_op | source)
XLA Modules:
  0.0 35.8 jit_solution(2013431108240863053)
XLA Ops:
  0.6 32.2 %fire_step.1 = (f32[4,8,64,128]{3,2,1,0:T(8,128)}, f32[24,1,256]{2,1,0:T(1,128)}) custom-call(f32[4,8,64,128]{3,2,1,0:T(8,128)} %fields_ref.1, f32[42,1,256]{2,1,0:T(1,128)} %bitcast.4, s32[1,1,6]{2,1,0:T(1,128)} %counts_ref.1), custom_call_target="tpu_custom_call" | custom-call | tf_op jit(solution)/shard_map/fire_step/pallas_call | solution.py:277
  32.8 0.0 copy-start
  32.8 2.3 %copy.8 = f32[4,8,64,128]{3,2,1,0:T(8,128)} copy(f32[4,8,64,128]{3,2,1,0:T(8,128)} %get-tuple-element.10) | data formatting | bytes 2097152
  35.2 0.0 copy-done
  35.2 0.6 %copy.9 = f32[4,1,1,6,256]{4,2,3,1,0:T(1,128)} copy(f32[4,1,1,6,256]{4,2,3,1,0:T(1,128)S(1)} %bitcast.5) | data formatting | bytes 49152
Async XLA Ops:
  32.8 2.3 %copy-start = (f32[24,1,256]{2,1,0:T(1,128)S(1)}, f32[24,1,256]{2,1,0:T(1,128)}, u32[]{:S(2)}) copy-start(f32[24,1,256]{2,1,0:T(1,128)} %get-tuple-element.5) | copy-start | bytes 73732

commit v4 on v3

--- a/solution.py
+++ b/solution.py
@@ -17,6 +17,8 @@
 DESTINATIONS = ((1, -1), (1, 0), (1, 1), (2, -1), (2, 0), (2, 1))
 PAD = 8
 CHUNK = 32
+BAND = 8
+INNER = 24
 MESH = pl.DeviceIdType.MESH
 
 
@@ -31,9 +33,9 @@
 
 
 def kernel(
-    nd, nc, fields_ref, embers_ref, counts_ref, advanced_ref, landed_ref,
-    state, ysend, yrecv, esend, erecv, split, spread, deposit, result,
-    in_sem, out_sem, edge_sem, x_send, x_recv, y_send, y_recv, e_send, e_recv,
+    nd, nc, fields_ref, embers_in, counts_in, advanced_ref, landed_ref, embers_ref, counts_ref,
+    state, ysend, yrecv, esend, erecv, split, spread, deposit,
+    in_sem, embers_sem, counts_sem, x_send, x_recv, y_send, y_recv, e_send, e_recv,
 ):
     fields, cx, cy, nz = fields_ref.shape
     slots, capacity = len(DESTINATIONS), embers_ref.shape[2]
@@ -48,6 +50,10 @@
 
     loading = pltpu.make_async_copy(fields_ref, state.at[0, :, pl.ds(1, cx), rows], in_sem)
     loading.start()
+    loading_embers = pltpu.make_async_copy(embers_in, embers_ref, embers_sem)
+    loading_embers.start()
+    loading_counts = pltpu.make_async_copy(counts_in, counts_ref, counts_sem)
+    loading_counts.start()
 
     zero_row = jnp.zeros((cy, nz), jnp.float32)
     for b in range(2):
@@ -68,6 +74,8 @@
         def _(a=a, b=b):
             pl.semaphore_signal(barrier, inc=1, device_id=(d + a, c + b), device_id_type=MESH)
 
+    loading_counts.wait()
+    loading_embers.wait()
     lane = lax.broadcasted_iota(jnp.int32, (1, capacity), 1)
     for j in range(slots):
         live = lane < counts_ref[0, 0, j]
@@ -138,31 +146,30 @@
     level = lax.broadcasted_iota(jnp.int32, (CHUNK, nz), 1)
     keep = 1.0 - 4.0 * HORIZONTAL_MIX - 2.0 * VERTICAL_MIX
 
-    def stencil(b, i, part, last):
-        for y in (part * CHUNK,):
-            here = slice(PAD + y, PAD + y + CHUNK)
-            u = state[b, 0, i, here, :] * (0.5 * ADVECTION)
-            v = state[b, 1, i, here, :] * (0.5 * ADVECTION)
-            for k in range(fields):
-                centre = state[b, k, i, here, :]
-                eastern = state[b, k, i + 1, here, :]
-                western = state[b, k, i - 1, here, :]
-                northern = state[b, k, i, PAD + y + 1:PAD + y + 1 + CHUNK, :]
-                southern = state[b, k, i, PAD + y - 1:PAD + y - 1 + CHUNK, :]
-                upper = jnp.where(level == nz - 1, centre, pltpu.roll(centre, nz - 1, 1))
-                lower = jnp.where(level == 0, centre, pltpu.roll(centre, 1, 1))
-                new = (
-                    keep * centre
-                    + HORIZONTAL_MIX * ((eastern + western) + (northern + southern))
-                    + VERTICAL_MIX * (upper + lower)
-                    - (u * (eastern - western) + v * (northern - southern))
-                )
-                if not last:
-                    state[1 - b, k, i, here, :] = new
-                else:
-                    if k == 2:
-                        new = new + deposit[pl.ds(pl.multiple_of((i - 1) * cy + y, CHUNK), CHUNK), :]
-                    result[k, i - 1, y:y + CHUNK, :] = new
+    def stencil(b, i, y, span, last):
+        here = slice(PAD + y, PAD + y + span)
+        u = state[b, 0, i, here, :] * (0.5 * ADVECTION)
+        v = state[b, 1, i, here, :] * (0.5 * ADVECTION)
+        for k in range(fields):
+            centre = state[b, k, i, here, :]
+            eastern = state[b, k, i + 1, here, :]
+            western = state[b, k, i - 1, here, :]
+            northern = state[b, k, i, PAD + y + 1:PAD + y + 1 + span, :]
+            southern = state[b, k, i, PAD + y - 1:PAD + y - 1 + span, :]
+            upper = jnp.where(level[:span] == nz - 1, centre, pltpu.roll(centre, nz - 1, 1))
+            lower = jnp.where(level[:span] == 0, centre, pltpu.roll(centre, 1, 1))
+            new = (
+                keep * centre
+                + HORIZONTAL_MIX * ((eastern + western) + (northern + southern))
+                + VERTICAL_MIX * (upper + lower)
+                - (u * (eastern - western) + v * (northern - southern))
+            )
+            if not last:
+                state[1 - b, k, i, here, :] = new
+            else:
+                if k == 2:
+                    new = new + deposit[pl.ds(pl.multiple_of((i - 1) * cy + y, BAND), span), :]
+                advanced_ref[k, i - 1, y:y + span, :] = new
 
     def embers_of(j):
         a, b = DESTINATIONS[j]
@@ -223,8 +230,6 @@
         split[at, cells:2 * cells] = high
         split[at, 2 * cells:] = low
 
-    inner_rows = pl.ds(1, cx - 2)
-    inner_out = pltpu.make_async_copy(result.at[:, inner_rows], advanced_ref.at[:, inner_rows], out_sem.at[0])
     for step in range(STEPS):
         b = step % 2
         last = step == STEPS - 1
@@ -234,27 +239,24 @@
             arrive_x(b, part)
             if step > 0:
                 sent_x(1 - b, part)
-            stencil(b, 1, part, last)
-            stencil(b, cx, part, last)
+            stencil(b, 1, part * CHUNK, CHUNK, last)
+            stencil(b, cx, part * CHUNK, CHUNK, last)
             if not last:
                 start_x(1 - b, part)
-            if part == 0:
-                def inner(i, carry, b=b, last=last):
-                    for part in range(parts):
-                        stencil(b, i, part, last)
-                    return carry
-
-                lax.fori_loop(2, cx, inner, 0)
-                if last:
-                    inner_out.start()
+        for i in range(2, cx):
+            stencil(b, i, 0, BAND, last)
+            stencil(b, i, cy - BAND, BAND, last)
         if step > 0:
             sent_y(1 - b)
         if not last:
             start_y(1 - b)
-    outer_out = []
-    for side, i in enumerate((0, cx - 1)):
-        outer_out.append(pltpu.make_async_copy(result.at[:, i], advanced_ref.at[:, i], edge_sem.at[side]))
-        outer_out[side].start()
+
+        def inner(i, carry, b=b, last=last):
+            for y in range(BAND, cy - BAND, INNER):
+                stencil(b, i, y, INNER, last)
+            return carry
+
+        lax.fori_loop(2, cx, inner, 0)
     for part in range(parts):
         sent_x((STEPS - 1) % 2, part)
     sent_y((STEPS - 1) % 2)
@@ -263,9 +265,16 @@
         def _(j=j):
             e_copy(j).wait_send()
 
-    inner_out.wait()
-    for copy in outer_out:
+def store(advanced_ref, landed_ref, advanced_out, landed_out, advanced_sem, landed_sem):
+    copies = (
+        pltpu.make_async_copy(advanced_ref, advanced_out, advanced_sem),
+        pltpu.make_async_copy(landed_ref, landed_out, landed_sem),
+    )
+    for copy in copies:
+        copy.start()
+    for copy in copies:
         copy.wait()
+
 
 def solution(mesh):
     nd, nc = mesh.shape["down"], mesh.shape["cross"]
@@ -273,20 +282,21 @@
     def local(fields, embers, counts):
         k, cx, cy, nz = fields.shape
         slots, capacity = embers.shape[3:]
+        arguments = (fields, embers.reshape(7 * slots, 1, capacity), counts)
         sem = pltpu.SemaphoreType.DMA
         advanced, landed = pl.pallas_call(
             functools.partial(kernel, nd, nc),
             out_shape=(
-                jax.ShapeDtypeStruct(fields.shape, jnp.float32),
-                jax.ShapeDtypeStruct((4 * slots, 1, capacity), jnp.float32),
+                pltpu.VMEM(fields.shape, jnp.float32),
+                pltpu.VMEM((4 * slots, 1, capacity), jnp.float32),
             ),
             in_specs=[
                 pl.BlockSpec(memory_space=pltpu.HBM),
-                pl.BlockSpec(memory_space=pltpu.VMEM),
-                pl.BlockSpec(memory_space=pltpu.SMEM),
-            ],
-            out_specs=[pl.BlockSpec(memory_space=pltpu.HBM), pl.BlockSpec(memory_space=pltpu.VMEM)],
+            ] * 3,
+            out_specs=[pl.BlockSpec(memory_space=pltpu.VMEM)] * 2,
             scratch_shapes=[
+                pltpu.VMEM((7 * slots, 1, capacity), jnp.float32),
+                pltpu.SMEM(counts.shape, jnp.int32),
                 pltpu.VMEM((2, k, cx + 2, cy + 2 * PAD, nz), jnp.float32),
                 pltpu.VMEM((2, 2, k, cx, nz), jnp.float32),
                 pltpu.VMEM((2, 2, k, cx, nz), jnp.float32),
@@ -295,15 +305,25 @@
                 pltpu.VMEM((k * nz, 3 * cx * cy), jnp.bfloat16),
                 pltpu.VMEM((3 * cx * cy, capacity), jnp.bfloat16),
                 pltpu.VMEM((cx * cy, nz), jnp.float32),
-                pltpu.VMEM(fields.shape, jnp.float32),
-                sem, sem((1,)), sem((2,)), sem((2, 2, cy // CHUNK)), sem((2, 2, cy // CHUNK)), sem((2, 2)), sem((2, 2)),
+                sem, sem, sem, sem((2, 2, cy // CHUNK)), sem((2, 2, cy // CHUNK)), sem((2, 2)), sem((2, 2)),
                 sem((slots,)), sem((slots,)),
             ],
             compiler_params=pltpu.CompilerParams(
-                collective_id=0, has_side_effects=True, vmem_limit_bytes=60 * 1024 * 1024
+                collective_id=0, has_side_effects=True, vmem_limit_bytes=40 * 1024 * 1024
             ),
             name="fire_step",
-        )(fields, embers.reshape(7 * slots, 1, capacity), counts)
+        )(*[pltpu.with_memory_space_constraint(x, pltpu.HBM) for x in arguments])
+        advanced, landed = pl.pallas_call(
+            store,
+            out_shape=(
+                jax.ShapeDtypeStruct(advanced.shape, jnp.float32),
+                jax.ShapeDtypeStruct(landed.shape, jnp.float32),
+            ),
+            in_specs=[pl.BlockSpec(memory_space=pl.ANY)] * 2,
+            out_specs=[pl.BlockSpec(memory_space=pltpu.HBM)] * 2,
+            scratch_shapes=[sem, sem],
+            name="store_results",
+        )(advanced, landed)
         return advanced, landed.reshape(4, 1, 1, slots, capacity)
 
     placed = (

time: 36 us -> 65.8 us (1.83)
  Pallas kernels: 32.2 us -> 63.5 us
  local copies, waits for them, and re-layouts: 2.92 us -> 1.57 us
    pallas_call x1 -> x2, Pallas kernels: 32.2 us -> 63.5 us  [the longest x1 33.6 us: local(): pl.pallas_call(store, out_shape=(jax.ShapeDtypeStruct(advanced.shape, jnp...]
    unnamed x4, local copies, waits for them, and re-layouts: 2.92 us -> 1.57 us
where the time goes in v4:
time: 65.8 us; the launch traced here: 65.7 us
  Pallas kernels  63.5 us (97%)
  local copies, waits for them, and re-layouts  1.57 us (2%)
    pallas_call x1, Pallas kernels, local(): pl.pallas_call(store, out_shape=(jax.ShapeDtypeStruct(advanced.shape, jnp...  33.6 us
    pallas_call x1, Pallas kernels, local(): pl.pallas_call(functools.partial(kernel, nd, nc), out_shape=(pltpu.VMEM(f...  29.8 us
    unnamed x4, local copies, waits for them, and re-layouts  1.57 us

profile of v4, /device:TPU:3, one launch (start us, length us, event | category | flops | bytes accessed | tf_op | source)
XLA Modules:
  0.0 65.7 jit_solution(8289612928910275381)
XLA Ops:
  0.6 29.8 %fire_step.1 = (f32[4,8,64,128]{3,2,1,0:T(8,128)S(1)}, f32[24,1,256]{2,1,0:T(1,128)S(1)}) custom-call(f32[4,8,64,128]{3,2,1,0:T(8,128)} %fields_ref.1, f32[42,1,256]{2,1,0:T(1,128)} %bitcast.4, s32[1,1,6]{2,1,0:T(1,128)} %counts_in.1), custom_call_target="tpu_custom_call" | custom-call | tf_op jit(solution)/shard_map/fire_step/pallas_call | solution.py:287
  30.5 0.0 copy-start
  30.5 1.0 %copy-done = f32[4,8,64,128]{3,2,1,0:T(8,128)} copy-done((f32[4,8,64,128]{3,2,1,0:T(8,128)}, f32[4,8,64,128]{3,2,1,0:T(8,128)S(1)}, u32[]{:S(2)}) %copy-start) | copy-done | bytes 1048600
  31.4 0.0 copy-start.1
  31.5 0.6 copy-done.1
  32.1 33.6 %store_results.1 = (f32[4,8,64,128]{3,2,1,0:T(8,128)}, f32[24,1,256]{2,1,0:T(1,128)}) custom-call(f32[4,8,64,128]{3,2,1,0:T(8,128)} %copy-done, f32[24,1,256]{2,1,0:T(1,128)} %copy-done.1), custom_call_target="tpu_custom_call" | custom-call | tf_op jit(solution)/shard_map/store_results/pallas_call | solution.py:316
Async XLA Ops:
  30.5 1.0 %copy-start = (f32[4,8,64,128]{3,2,1,0:T(8,128)}, f32[4,8,64,128]{3,2,1,0:T(8,128)S(1)}, u32[]{:S(2)}) copy-start(f32[4,8,64,128]{3,2,1,0:T(8,128)S(1)} %get-tuple-element.6.advanced_ref) | copy-start | bytes 3145732
  31.4 0.6 copy-start.1

commit v5 on v4

--- a/solution.py
+++ b/solution.py
@@ -16,7 +16,7 @@
 HEAT_YIELD = 4.0
 DESTINATIONS = ((1, -1), (1, 0), (1, 1), (2, -1), (2, 0), (2, 1))
 PAD = 8
-CHUNK = 32
+OUTER = 16
 BAND = 8
 INNER = 24
 MESH = pl.DeviceIdType.MESH
@@ -42,7 +42,7 @@
     d = lax.axis_index("down")
     c = lax.axis_index("cross")
     rows = pl.ds(PAD, cy)
-    parts = cy // CHUNK
+    segments = ((0, OUTER), (cy - OUTER, OUTER), (OUTER, cy - 2 * OUTER))
     cells = cx * cy
 
     def inside(a, b):
@@ -85,7 +85,7 @@
 
     def x_copy(b, side, part):
         source, target, by = ((cx, 0, 1), (1, cx + 1, -1))[side]
-        band = pl.ds(PAD + part * CHUNK, CHUNK)
+        band = pl.ds(PAD + segments[part][0], segments[part][1])
         return pltpu.make_async_remote_copy(
             src_ref=state.at[b, :, source, band],
             dst_ref=state.at[b, :, target, band],
@@ -143,7 +143,7 @@
                 state[b, k, i + 1, PAD - 1:PAD, :] = yrecv[b, 0, k, i:i + 1, :]
                 state[b, k, i + 1, PAD + cy:PAD + cy + 1, :] = yrecv[b, 1, k, i:i + 1, :]
 
-    level = lax.broadcasted_iota(jnp.int32, (CHUNK, nz), 1)
+    level = lax.broadcasted_iota(jnp.int32, (32, nz), 1)
     keep = 1.0 - 4.0 * HORIZONTAL_MIX - 2.0 * VERTICAL_MIX
 
     def stencil(b, i, y, span, last):
@@ -219,30 +219,35 @@
             e_copy(j).start()
     loading.wait()
 
-    for part in range(parts):
-        start_x(0, part)
+    start_x(0, 0)
+    start_x(0, 1)
     start_y(0)
-    for k in range(fields):
-        at = slice(k * nz, (k + 1) * nz)
-        own = state[0, k, 1:cx + 1, PAD:PAD + cy, :].reshape(cells, nz)
-        high, low = halves(own.T)
-        split[at, :cells] = high
-        split[at, cells:2 * cells] = high
-        split[at, 2 * cells:] = low
+    start_x(0, 2)
 
     for step in range(STEPS):
         b = step % 2
         last = step == STEPS - 1
-        embers_of(step)
-        arrive_y(b)
-        for part in range(parts):
+
+        def edges(part, b=b, step=step, last=last):
             arrive_x(b, part)
             if step > 0:
                 sent_x(1 - b, part)
-            stencil(b, 1, part * CHUNK, CHUNK, last)
-            stencil(b, cx, part * CHUNK, CHUNK, last)
+            y, span = segments[part]
+            stencil(b, 1, y, span, last)
+            stencil(b, cx, y, span, last)
             if not last:
                 start_x(1 - b, part)
+
+        def inner(i, carry, b=b, last=last):
+            for y in range(BAND, cy - BAND, INNER):
+                stencil(b, i, y, INNER, last)
+            return carry
+
+        if last:
+            embers_of(step)
+        arrive_y(b)
+        edges(0)
+        edges(1)
         for i in range(2, cx):
             stencil(b, i, 0, BAND, last)
             stencil(b, i, cy - BAND, BAND, last)
@@ -250,31 +255,25 @@
             sent_y(1 - b)
         if not last:
             start_y(1 - b)
-
-        def inner(i, carry, b=b, last=last):
-            for y in range(BAND, cy - BAND, INNER):
-                stencil(b, i, y, INNER, last)
-            return carry
-
         lax.fori_loop(2, cx, inner, 0)
-    for part in range(parts):
+        if step == 0:
+            for k in range(fields):
+                at = slice(k * nz, (k + 1) * nz)
+                own = state[0, k, 1:cx + 1, PAD:PAD + cy, :].reshape(cells, nz)
+                high, low = halves(own.T)
+                split[at, :cells] = high
+                split[at, cells:2 * cells] = high
+                split[at, 2 * cells:] = low
+        if not last:
+            embers_of(step)
+        edges(2)
+    for part in range(len(segments)):
         sent_x((STEPS - 1) % 2, part)
     sent_y((STEPS - 1) % 2)
     for j in range(slots):
         @pl.when(inside(*DESTINATIONS[j]))
         def _(j=j):
             e_copy(j).wait_send()
-
-def store(advanced_ref, landed_ref, advanced_out, landed_out, advanced_sem, landed_sem):
-    copies = (
-        pltpu.make_async_copy(advanced_ref, advanced_out, advanced_sem),
-        pltpu.make_async_copy(landed_ref, landed_out, landed_sem),
-    )
-    for copy in copies:
-        copy.start()
-    for copy in copies:
-        copy.wait()
-
 
 def solution(mesh):
     nd, nc = mesh.shape["down"], mesh.shape["cross"]
@@ -305,7 +304,7 @@
                 pltpu.VMEM((k * nz, 3 * cx * cy), jnp.bfloat16),
                 pltpu.VMEM((3 * cx * cy, capacity), jnp.bfloat16),
                 pltpu.VMEM((cx * cy, nz), jnp.float32),
-                sem, sem, sem, sem((2, 2, cy // CHUNK)), sem((2, 2, cy // CHUNK)), sem((2, 2)), sem((2, 2)),
+                sem, sem, sem, sem((2, 2, 3)), sem((2, 2, 3)), sem((2, 2)), sem((2, 2)),
                 sem((slots,)), sem((slots,)),
             ],
             compiler_params=pltpu.CompilerParams(
@@ -313,17 +312,6 @@
             ),
             name="fire_step",
         )(*[pltpu.with_memory_space_constraint(x, pltpu.HBM) for x in arguments])
-        advanced, landed = pl.pallas_call(
-            store,
-            out_shape=(
-                jax.ShapeDtypeStruct(advanced.shape, jnp.float32),
-                jax.ShapeDtypeStruct(landed.shape, jnp.float32),
-            ),
-            in_specs=[pl.BlockSpec(memory_space=pl.ANY)] * 2,
-            out_specs=[pl.BlockSpec(memory_space=pltpu.HBM)] * 2,
-            scratch_shapes=[sem, sem],
-            name="store_results",
-        )(advanced, landed)
         return advanced, landed.reshape(4, 1, 1, slots, capacity)
 
     placed = (

time: 65.8 us -> 31.4 us (0.48)
  Pallas kernels: 63.5 us -> 29 us
    pallas_call x1 -> x0, Pallas kernels: 33.6 us -> none  [local(): pl.pallas_call(store, out_shape=(jax.ShapeDtypeStruct(advanced.shape, jnp...]
    pallas_call x1, Pallas kernels: 29.8 us -> 29 us  [local(): pl.pallas_call(functools.partial(kernel, nd, nc), out_shape=(pltpu.VMEM(f...]
    unnamed x4 -> x2, local copies, waits for them, and re-layouts: 1.57 us -> 1.58 us
where the time goes in v5:
time: 31.4 us; the launch traced here: 31.2 us
  Pallas kernels  29 us (92%)
  local copies, waits for them, and re-layouts  1.58 us (5%)
  between operations  0.64 us (2%)
    pallas_call x1, Pallas kernels, local(): pl.pallas_call(functools.partial(kernel, nd, nc), out_shape=(pltpu.VMEM(f...  29 us
    unnamed x2, local copies, waits for them, and re-layouts  1.58 us

profile of v5, /device:TPU:3, one launch (start us, length us, event | category | flops | bytes accessed | tf_op | source)
XLA Modules:
  0.0 31.2 jit_solution(13764336604512713563)
XLA Ops:
  0.6 29.0 %fire_step.1 = (f32[4,8,64,128]{3,2,1,0:T(8,128)S(1)}, f32[24,1,256]{2,1,0:T(1,128)S(1)}) custom-call(f32[4,8,64,128]{3,2,1,0:T(8,128)} %fields_ref.1, f32[42,1,256]{2,1,0:T(1,128)} %bitcast.5, s32[1,1,6]{2,1,0:T(1,128)} %counts_in.1), custom_call_target="tpu_custom_call" | custom-call | tf_op jit(solution)/shard_map/fire_step/pallas_call | solution.py:286
  29.7 1.0 %copy.8 = f32[4,8,64,128]{3,2,1,0:T(8,128)} copy(f32[4,8,64,128]{3,2,1,0:T(8,128)S(1)} %get-tuple-element.8) | data formatting | bytes 2097152
  30.6 0.6 %copy.9 = f32[4,1,1,6,256]{4,2,3,1,0:T(1,128)} copy(f32[4,1,1,6,256]{4,2,3,1,0:T(1,128)S(1)} %bitcast.4) | data formatting | bytes 49152

commit v6 on v5

--- a/solution.py
+++ b/solution.py
@@ -223,6 +223,14 @@
     start_x(0, 1)
     start_y(0)
     start_x(0, 2)
+    for k in range(fields):
+        at = slice(k * nz, (k + 1) * nz)
+        own = state[0, k, 1:cx + 1, PAD:PAD + cy, :].reshape(cells, nz)
+        high, low = halves(own.T)
+        split[at, :cells] = high
+        split[at, cells:2 * cells] = high
+        split[at, 2 * cells:] = low
+    embers_of(0)
 
     for step in range(STEPS):
         b = step % 2
@@ -243,8 +251,6 @@
                 stencil(b, i, y, INNER, last)
             return carry
 
-        if last:
-            embers_of(step)
         arrive_y(b)
         edges(0)
         edges(1)
@@ -256,17 +262,9 @@
         if not last:
             start_y(1 - b)
         lax.fori_loop(2, cx, inner, 0)
-        if step == 0:
-            for k in range(fields):
-                at = slice(k * nz, (k + 1) * nz)
-                own = state[0, k, 1:cx + 1, PAD:PAD + cy, :].reshape(cells, nz)
-                high, low = halves(own.T)
-                split[at, :cells] = high
-                split[at, cells:2 * cells] = high
-                split[at, 2 * cells:] = low
+        edges(2)
         if not last:
-            embers_of(step)
-        edges(2)
+            embers_of(step + 1)
     for part in range(len(segments)):
         sent_x((STEPS - 1) % 2, part)
     sent_y((STEPS - 1) % 2)

time: 31.4 us -> 30.4 us (0.968)
  Pallas kernels: 29 us -> 27.7 us
    pallas_call x1, Pallas kernels: 29 us -> 27.7 us  [local(): pl.pallas_call(functools.partial(kernel, nd, nc), out_shape=(pltpu.VMEM(f...]
where the time goes in v6:
time: 30.4 us; the launch traced here: 30 us
  Pallas kernels  27.7 us (91%)
  local copies, waits for them, and re-layouts  1.58 us (5%)
  between operations  0.64 us (2%)
    pallas_call x1, Pallas kernels, local(): pl.pallas_call(functools.partial(kernel, nd, nc), out_shape=(pltpu.VMEM(f...  27.7 us
    unnamed x2, local copies, waits for them, and re-layouts  1.58 us

profile of v6, /device:TPU:3, one launch (start us, length us, event | category | flops | bytes accessed | tf_op | source)
XLA Modules:
  0.0 30.0 jit_solution(12883675484731061396)
XLA Ops:
  0.6 27.7 %fire_step.1 = (f32[4,8,64,128]{3,2,1,0:T(8,128)S(1)}, f32[24,1,256]{2,1,0:T(1,128)S(1)}) custom-call(f32[4,8,64,128]{3,2,1,0:T(8,128)} %fields_ref.1, f32[42,1,256]{2,1,0:T(1,128)} %bitcast.5, s32[1,1,6]{2,1,0:T(1,128)} %counts_in.1), custom_call_target="tpu_custom_call" | custom-call | tf_op jit(solution)/shard_map/fire_step/pallas_call | solution.py:284
  28.4 1.0 %copy.8 = f32[4,8,64,128]{3,2,1,0:T(8,128)} copy(f32[4,8,64,128]{3,2,1,0:T(8,128)S(1)} %get-tuple-element.8) | data formatting | bytes 2097152
  29.3 0.6 %copy.9 = f32[4,1,1,6,256]{4,2,3,1,0:T(1,128)} copy(f32[4,1,1,6,256]{4,2,3,1,0:T(1,128)S(1)} %bitcast.4) | data formatting | bytes 49152
